TPU v7x, 256 devices: a whole 4x4x8 slice. The times are simulated.
256 devices in a mesh: dp: 32 (over y_hi, z, core), tensor: 8 (over x, y_lo).
Axes of the slice: x: 4, y: 4 (y_hi: 2, y_lo: 2; y = y_hi * 2 + y_lo), z: 8, core: 2. Of those that a mesh axis runs over, the one named last changes fastest.
Arguments:
- activations: bfloat16 [16384, 8192], P('dp', 'tensor'), may hold values from -6 to 6
- cotangent: bfloat16 [16384, 1024], P('dp', 'tensor'), may hold values from -6 to 6
- weight: bfloat16 [8192, 1024], P(None, 'tensor'), may hold values from -0.0625 to 0.0625
- momentum: float32 [32, 8192, 1024], P('dp', None, 'tensor'), may hold values from -24 to 24
- band_anchor: int32 [128, 16, 2], P(None, 'tensor'), may hold values from 0 to 8
Outputs:
- input_grad: bfloat16 [16384, 8192], P('dp', 'tensor')
- new_momentum: float32 [32, 8192, 1024], P('dp', None, 'tensor')
- weight_step: bfloat16 [8192, 1024], P(None, 'tensor')
Inputs may be any that keep to these rules, and one draw needn't show every extreme that they name: `band_anchor`: for every group the band of 8 x 8 frequencies from this anchor lies inside the group; all workers share the anchors.
All inputs are finite; a program needn't handle non-finite values.
Results may differ from a plain program's by a relative error of at most 0.001.
Values may be sent and summed in bfloat16 or wider, within the bound.
No kernel may reach another device: no remote copies, remote signals or barrier semaphores. Data moves between devices by JAX's collectives and lax.ppermute only.
A program may use at most 128 MiB of HBM per device.

v0:
```python
import jax
import jax.numpy as jnp
from jax import lax
from jax.sharding import PartitionSpec as P

GROUP = 64
BAND = 8


PRECISE = lax.Precision.HIGHEST
MOMENTUM_DECAY = 0.9


def cosine_basis(length):
    freq_index = jnp.arange(length, dtype=jnp.float32)[:, None]
    cell_index = jnp.arange(length, dtype=jnp.float32)[None, :]
    norm_scale = jnp.where(freq_index == 0, jnp.sqrt(1.0 / length), jnp.sqrt(2.0 / length))
    return norm_scale * jnp.cos(jnp.pi * (2.0 * cell_index + 1.0) * freq_index / (2.0 * length))


def band_bases(band_anchor):
    col_groups = band_anchor.shape[1]
    cosine_table = cosine_basis(GROUP)
    offsets = jnp.arange(BAND, dtype=jnp.int32)
    frequency = jnp.arange(GROUP, dtype=jnp.int32)
    row_select = (band_anchor[:, :, 0, None, None] + offsets[:, None] == frequency).astype(
        jnp.float32
    )
    col_select = (band_anchor[:, :, 1, None, None] + offsets[:, None] == frequency).astype(
        jnp.float32
    )
    row_basis = jnp.einsum("klif,fa->klia", row_select, cosine_table, precision=PRECISE)
    col_basis = jnp.einsum("kljf,fb->kljb", col_select, cosine_table, precision=PRECISE)
    column = jnp.arange(col_groups * GROUP, dtype=jnp.int32)
    owner_mask = (column // GROUP == jnp.arange(col_groups, dtype=jnp.int32)[:, None]).astype(
        jnp.float32
    )
    spread = jnp.tile(col_basis, (1, 1, 1, col_groups))
    wide_basis = spread * owner_mask[None, :, None, :]
    return (row_basis, wide_basis)


def analyse(moment, row_basis, wide_basis):
    blocks = moment.reshape(row_basis.shape[0], GROUP, moment.shape[1])
    projected = jnp.einsum("kac,kljc->klja", blocks, wide_basis, precision=PRECISE)
    return jnp.einsum("klia,klja->klij", row_basis, projected, precision=PRECISE)


def rebuild(low_band, row_basis, wide_basis):
    partial_value = jnp.einsum("klij,kljc->klic", low_band, wide_basis, precision=PRECISE)
    blocks = jnp.einsum("klia,klic->kac", row_basis, partial_value, precision=PRECISE)
    return blocks.reshape(-1, wide_basis.shape[-1])


def body(activations, cotangent, weight, momentum, band_anchor):
    weight_grad = lax.dot_general(
        lax.all_gather(activations, "tensor", axis=1, tiled=True),
        cotangent,
        (((0,), (0,)), ((), ())),
        preferred_element_type=jnp.float32,
    )
    input_terms = lax.dot_general(
        cotangent, weight, (((1,), (1,)), ((), ())), preferred_element_type=jnp.float32
    )
    input_grad = lax.psum_scatter(input_terms, "tensor", scatter_dimension=1, tiled=True).astype(
        jnp.bfloat16
    )
    moment = MOMENTUM_DECAY * momentum[0] + weight_grad
    row_basis, wide_basis = band_bases(band_anchor)
    low_band = analyse(moment, row_basis, wide_basis)
    new_momentum = (moment - rebuild(low_band, row_basis, wide_basis))[None]
    band_total = lax.psum(low_band, "dp")
    weight_step = rebuild(band_total, row_basis, wide_basis).astype(jnp.bfloat16)
    return (input_grad, new_momentum, weight_step)


def solution(mesh):
    return jax.shard_map(
        body,
        mesh=mesh,
        in_specs=(
            P("dp", "tensor"),
            P("dp", "tensor"),
            P(None, "tensor"),
            P("dp", None, "tensor"),
            P(None, "tensor", None),
        ),
        out_specs=(P("dp", "tensor"), P("dp", None, "tensor"), P(None, "tensor")),
        check_vma=False,
    )
```

profile of v0, /device:TPU:1, one launch (start us, length us, event | category | flops | bytes accessed | tf_op | source)
XLA Modules:
  0.0 824.2 jit_solution(6675901465387975758)
XLA Ops:
  7.2 0.0 all-gather.2.cloned.1.call-start
  7.2 0.7 all-gather.2.cloned.1.call-update
  7.9 0.8 fusion.14
  8.7 0.6 fusion
  9.3 1.4 copy.13
  10.7 0.6 fusion.1
  11.2 1.2 bitcast_multiply_fusion
  12.4 1.7 copy.16
  14.1 170.4 %all-gather.2.cloned.1.call-done = bf16[512,8192]{1,0:T(8,128)(2,1)} async-done(((bf16[512,1024]{1,0:T(8,128)(2,1)}), bf16[512,8192]{1,0:T(8,128)(2,1)}) %all-gather.2.cloned.1.call-update) | async-done | bytes 8388624 | tf_op jit(solution)/shard_map/all_gather | solution.py:57
  184.6 7.0 convolution_add_fusion
  191.5 2.0 copy-done.1
  193.5 6.6 fusion.16
  200.1 2.8 fusion.17
  202.9 4.2 fusion.18
  207.1 0.7 all-reduce.2.cloned.1.call-update
  207.8 0.0 reduce-scatter.2.cloned.1.call-start
  207.9 8.1 fusion.15
  216.0 8.5 %fusion.19 = f32[128,64,128,1]{2,1,3,0:T(8,128)S(1)} fusion(f32[128,2,8,64]{3,2,1,0:T(8,128)} %copy.13, f32[128,2,8,128]{3,2,1,0:T(8,128)} %fusion.18), kind=kOutput, calls=%fused_computation.35 | convolution fusion | flops 201326592 | bytes 5767168 | tf_op jit(solution)/shard_map/klia,klic->kac/dot_general | solution.py:51
  224.5 2.4 bitcast_subtract_fusion
  226.9 257.7 %all-reduce.2.cloned.1.call-done = f32[128,2,8,8]{3,2,1,0:T(8,128)} async-done(((f32[128,2,8,8]{3,2,1,0:T(8,128)}), f32[128,2,8,8]{3,2,1,0:T(8,128)}) %all-reduce.2.cloned.1.call-update) | async-done | bytes 65552 | tf_op jit(solution)/shard_map/psum | solution.py:72
  484.7 3.0 fusion.20
  487.7 9.2 %bitcast_convert_fusion = bf16[128,64,128]{2,1,0:T(8,128)(2,1)} fusion(f32[128,2,8,64]{3,2,1,0:T(8,128)} %copy.13, f32[128,2,8,128]{3,2,1,0:T(8,128)S(1)} %fusion.20), kind=kOutput, calls=%fused_computation.2 | convolution fusion | flops 202375168 | bytes 3670016 | tf_op jit(solution)/shard_map/klia,klic->kac/dot_general | solution.py:51
  496.9 318.1 %reduce-scatter.2.cloned.1.call-done = f32[512,1024]{1,0:T(8,128)} async-done(((f32[512,8192]{1,0:T(8,128)}), f32[512,1024]{1,0:T(8,128)}) %reduce-scatter.2.cloned.1.call-update) | async-done | bytes 2097168 | tf_op jit(solution)/shard_map/reduce_scatter | solution.py:65
  815.0 2.7 convert_element_type.18
  (16 shorter events, 0.1 us)
Async XLA Ops:
  7.2 200.7 %copy-start = (bf16[8192,128]{1,0:T(8,128)(2,1)S(1)}, bf16[8192,128]{1,0:T(8,128)(2,1)}, u32[]{:S(2)}) copy-start(bf16[8192,128]{1,0:T(8,128)(2,1)} %param.7) | copy-start | bytes 6291460
  7.2 177.4 %copy-start.4 = (bf16[512,128]{1,0:T(8,128)(2,1)S(1)}, bf16[512,128]{1,0:T(8,128)(2,1)}, u32[]{:S(2)}) copy-start(bf16[512,128]{1,0:T(8,128)(2,1)} %param.6) | copy-start | bytes 393220
  7.2 177.4 %all-gather.2.cloned.1.call-start = ((), (), s32[]{:S(2)}) async-start(), calls=%async_computation.2 | async-start | bytes 9437184 | tf_op jit(solution)/shard_map/all_gather | solution.py:57
  191.5 2.0 copy-start.1
  191.5 8.6 %copy-start.3 = (f32[128,2,8,64]{3,2,1,0:T(8,128)S(1)}, f32[128,2,8,64]{3,2,1,0:T(8,128)}, u32[]{:S(2)}) copy-start(f32[128,2,8,64]{3,2,1,0:T(8,128)} %copy.13) | copy-start | bytes 1572868
  207.1 277.6 %all-reduce.2.cloned.1.call-start = ((), (), s32[]{:S(2)}) async-start(), calls=%async_computation.3 | async-start | bytes 2097152 | tf_op jit(solution)/shard_map/psum | solution.py:72
  207.8 607.1 %reduce-scatter.2.cloned.1.call-start = ((), (), s32[]{:S(2)}) async-start(), calls=%async_computation.1 | async-start | bytes 18874368 | tf_op jit(solution)/shard_map/reduce_scatter | solution.py:65
  216.0 8.5 %copy-start.2 = (f32[8192,128]{1,0:T(8,128)S(1)}, f32[8192,128]{1,0:T(8,128)}, u32[]{:S(2)}) copy-start(f32[8192,128]{1,0:T(8,128)} %copy-done.1) | copy-start | bytes 12582916
Sparse Core Ops, SparseCore 0:
  9.8 174.6 all-gather.1
  211.1 273.4 all-reduce.1
  487.5 327.4 reduce-scatter.1
where the time goes:
time: 824 us
  waiting for transfers between devices  748 us (91%)
  matrix products  50.4 us (6%)
  between operations  13.8 us (2%)
    reduce_scatter x1, waiting for transfers between devices, body(): lax.psum_scatter(input_terms, 'tensor', scatter_dimension=1, tiled=True)  318 us
    psum x1, waiting for transfers between devices, body(): band_total = lax.psum(low_band, 'dp')  258 us
    all_gather x1, waiting for transfers between devices, body(): lax.all_gather(activations, 'tensor', axis=1, tiled=True)  170 us
    dot_general x2, matrix products, rebuild(): jnp.einsum('klia,klic->kac', row_basis, partial_value, precision=PRECISE)  17.7 us
  transfers between devices with their start and end apart: 3, of which 3 were waited for; matrix products, arithmetic and copies ran while one was open for 5% of the time, Pallas kernels for 0%

commit v1 on v0

v1 whole, which is shorter than its diff:
```python
import functools

import jax
import jax.numpy as jnp
import numpy as np
from jax import lax
from jax.experimental import pallas as pl
from jax.experimental.pallas import tpu as pltpu
from jax.sharding import Mesh
from jax.sharding import PartitionSpec as P

GROUP = 64
BAND = 8
FREQ = 16
DECAY = 0.9
LIMIT = 20.0

F32, BF16, F16 = jnp.float32, jnp.bfloat16, jnp.float16
TENSOR = ("x", "yl")
NT = (((1,), (1,)), ((), ()))


def split_const(a):
    a = np.asarray(a, np.float32)
    hi = a.astype(jnp.bfloat16)
    lo = (a - hi.astype(np.float32)).astype(jnp.bfloat16)
    return hi, lo


def tables():
    f = np.arange(FREQ)[:, None]
    a = np.arange(GROUP)[None, :]
    scale = np.where(f == 0, np.sqrt(1 / GROUP), np.sqrt(2 / GROUP))
    c16 = scale * np.cos(np.pi * (2 * a + 1) * f / (2 * GROUP))
    rows = np.kron(np.eye(4), c16)
    cols = np.tile(np.kron(np.eye(2), c16.T), (1, 4))
    rh, rl = split_const(rows)
    th, tl = split_const(rows.T)
    ch, cl = split_const(cols)
    uh, ul = split_const(cols.T)
    place = [
        np.kron(np.kron(np.eye(8), pick), np.ones((1, FREQ)))
        for pick in ([[1], [0]], [[0], [1]])
    ]
    return np.concatenate(
        [
            rh,
            rl,
            np.concatenate([th, tl, th, np.zeros_like(th)], axis=1),
            np.concatenate([ch, cl], axis=1),
            np.concatenate([uh, ul], axis=1),
            np.concatenate(place, axis=1).astype(rh.dtype),
        ],
        axis=0,
    )


ROWS = slice(0, 128)
ROWS_T = slice(128, 384)
COLS = slice(384, 512)
COLS_T = slice(512, 640)
PLACE = slice(640, 656)


def split(a):
    hi = a.astype(BF16)
    return hi, (a - hi.astype(F32)).astype(BF16)


def mm(a, b):
    return jnp.dot(a, b, preferred_element_type=F32)


def times_table(a, table):
    hi, lo = split(a)
    both = mm(hi, table)
    return both[:, :128] + (both[:, 128:] + mm(lo, table[:, :128]))


def lane_block(shape, kk):
    lane = lax.broadcasted_iota(jnp.int32, shape, len(shape) - 1)
    return lane // 32 == kk


def pick_lanes(parts):
    out = parts[0]
    for kk in range(1, 4):
        out = jnp.where(lane_block(out.shape, kk), parts[kk], out)
    return out


def moment_band_kernel(m_ref, table_ref, o_ref):
    z = []
    for q in range(4):
        m = jnp.concatenate(split(m_ref[q * 256 : (q + 1) * 256, :]), axis=1)
        v = mm(table_ref[ROWS, :], m)
        z.append(v[:64, :128] + (v[:64, 128:] + v[64:, :128]))
    y = times_table(jnp.concatenate(z, axis=0), table_ref[COLS, :])
    for q in range(4):
        o_ref[0, q * 16 : (q + 1) * 16, :] = pick_lanes(
            [y[q * 64 + kk * 16 : q * 64 + (kk + 1) * 16] for kk in range(4)]
        )


def grad_band_kernel(a_ref, cot_ref, table_ref, o_ref):
    high, low = [], []
    for q in range(4):
        v = lax.dot_general(
            table_ref[ROWS, :], a_ref[:, q * 256 : (q + 1) * 256], NT, preferred_element_type=F32
        )
        h, l = split(v[:64] + v[64:])
        high.append(h)
        low.append(l)
    high, low = jnp.concatenate(high, axis=0), jnp.concatenate(low, axis=0)
    for j in range(0, 8, 2):
        halves = []
        for i in (j, j + 1):
            both = mm(cot_ref[i, :512, :], table_ref[COLS, :])
            halves.append(split(both[:, :128] + both[:, 128:]))
        rh = jnp.concatenate([halves[0][0], halves[1][0]], axis=1)
        rl = jnp.concatenate([halves[0][1], halves[1][1]], axis=1)
        x = mm(high, rh) + (mm(high, rl) + mm(low, rh))
        for i in (0, 1):
            for q in range(4):
                o_ref[j + i, q * 16 : (q + 1) * 16, :] = pick_lanes(
                    [
                        x[q * 64 + kk * 16 : q * 64 + (kk + 1) * 16, i * 128 : (i + 1) * 128]
                        for kk in range(4)
                    ]
                )


def band_mask(anchor, place):
    at = mm(anchor, place)
    r, c = at[:, None, :128], at[:, None, 128:]
    shape = (32, FREQ, 128)
    f = lax.broadcasted_iota(jnp.int32, shape, 1).astype(F32)
    g = (lax.broadcasted_iota(jnp.int32, shape, 2) % FREQ).astype(F32)
    inside = (f >= r) & (f < r + BAND) & (g >= c) & (g < c + BAND)
    return jnp.where(inside, 1.0, 0.0).astype(F32)


def pack_kernel(xm_ref, xg_ref, a_ref, table_ref, low_ref, pack_ref):
    mask = band_mask(a_ref[...], table_ref[PLACE, :]).reshape(8, 64, 128)
    low = mask * (xg_ref[...] + DECAY * xm_ref[...])
    low_ref[...] = low
    rows = low.reshape(8, 4, 2, 8, 128)
    rows = (rows[:, :, 0] + rows[:, :, 1]).reshape(2, 128, 128)
    a, b = rows[0], rows[1]
    lane = lax.broadcasted_iota(jnp.int32, a.shape, 1)
    pack_ref[...] = jnp.where(lane % 16 < 8, a + pltpu.roll(a, 120, 1), b + pltpu.roll(b, 8, 1))


def unpack(p, mask):
    lane = lax.broadcasted_iota(jnp.int32, p.shape, 1)
    low = lane % 16 < 8
    a = jnp.where(low, p, pltpu.roll(p, 8, 1))
    b = jnp.where(low, pltpu.roll(p, 120, 1), p)
    r = jnp.concatenate([a, b], axis=0).reshape(8, 4, 1, 8, 128)
    r = jnp.broadcast_to(r, (8, 4, 2, 8, 128)).reshape(8, 64, 128)
    return r * mask


def rebuild_chunk(low, table_ref):
    spread = []
    for q in range(4):
        part = low[q * 16 : (q + 1) * 16]
        spread += [jnp.where(lane_block(part.shape, kk), part, 0.0) for kk in range(4)]
    v = times_table(jnp.concatenate(spread, axis=0), table_ref[COLS_T, :])
    out = []
    for q in (0, 2):
        pair = jnp.concatenate([v[q * 64 : (q + 1) * 64], v[(q + 1) * 64 : (q + 2) * 64]], axis=1)
        hi, lo = split(pair)
        both = mm(table_ref[ROWS_T, :192], jnp.concatenate([hi, hi, lo], axis=0))
        out += [both[:, :128], both[:, 128:]]
    return out


def rest_kernel(low_ref, m_ref, table_ref, o_ref):
    for q, v in enumerate(rebuild_chunk(low_ref[0], table_ref)):
        rows = slice(q * 256, (q + 1) * 256)
        o_ref[0, rows, :] = DECAY * m_ref[rows, :] - v


def step_kernel(pack_ref, a_ref, table_ref, o_ref, low_ref):
    @pl.when(pl.program_id(0) == 0)
    def _():
        mask = band_mask(a_ref[...], table_ref[PLACE, :]).reshape(8, 64, 128)
        low_ref[...] = unpack(pack_ref[...], mask)

    for q, v in enumerate(rebuild_chunk(low_ref[pl.program_id(0)], table_ref)):
        o_ref[q * 256 : (q + 1) * 256, :] = v.astype(BF16)


def input_kernel(cot_ref, w_ref, o_ref):
    lhs = jnp.concatenate([cot_ref[j, :512, :] for j in range(8)], axis=1)
    count, _, part, _ = w_ref.shape
    step = max(1, 256 // part)
    size = step * part
    for i in range(0, count, step):
        rhs = jnp.concatenate(
            [w_ref[i : i + step, j].reshape(size, 128) for j in range(8)], axis=1
        )
        v = lax.dot_general(lhs, rhs, NT, preferred_element_type=F32)
        o_ref[:, i * part : i * part + size] = v.astype(BF16)


def whole(a):
    return pl.BlockSpec(a.shape, lambda i: (0,) * a.ndim)


def params(mib=16):
    return pltpu.CompilerParams(vmem_limit_bytes=mib * 2**20)


def cost(mflops, kib):
    return pl.CostEstimate(
        flops=mflops * 10**6, bytes_accessed=kib * 2**10, transcendentals=0
    )


def exchange_sum(v, axes, sizes, moves):
    n = int(np.prod([sizes[a] for a in axes]))
    moves = [m for m in moves if m < n]
    got = [lax.ppermute(v, axes, [(i, i ^ m) for i in range(n)]) for m in moves]
    if len(got) == 3:
        return (v + got[0]) + (got[1] + got[2])
    return v + got[0] if got else v


def body(sizes, activations, cotangent, weight, momentum, band_anchor):
    table = jnp.asarray(tables())
    nz, nc = sizes["z"], sizes["c"]
    moment0 = momentum[0]
    anchor = band_anchor.reshape(32, 16).astype(BF16)

    part = 1024 // (nz * nc)
    with jax.named_scope("gather_cotangent"):
        at = (lax.axis_index("z") * nc + lax.axis_index("c")) * part
        mine = lax.dynamic_slice(weight.reshape(8, 1024, 128), (0, at, 0), (8, part, 128))
        sent = jnp.concatenate([jnp.broadcast_to(cotangent, (8, 512, 128)), mine], axis=1)
        got = lax.all_to_all(sent, TENSOR, 0, 0)

    with jax.named_scope("share_weight"):
        rows_all = lax.all_gather(got[:, 512:], ("z", "c"))

    with jax.named_scope("moment_band"):
        moment_band = pl.pallas_call(
            moment_band_kernel,
            grid=(8,),
            in_specs=[pl.BlockSpec((1024, 128), lambda i: (i, 0)), whole(table)],
            out_specs=pl.BlockSpec((1, 64, 128), lambda i: (i, 0, 0)),
            out_shape=jax.ShapeDtypeStruct((8, 64, 128), F32),
            compiler_params=params(),
            cost_estimate=cost(2000, 4096),
        )(moment0, table)

    own_scale = jnp.maximum(jnp.max(jnp.abs(cotangent), axis=0).astype(F32), 1e-30) / LIMIT

    with jax.named_scope("grad_band"):
        grad_band = pl.pallas_call(
            grad_band_kernel,
            out_shape=jax.ShapeDtypeStruct((8, 64, 128), F32),
            compiler_params=params(),
            cost_estimate=cost(2000, 2048),
        )(activations, got, table)
        got, grad_band = lax.optimization_barrier((got, grad_band))
        grad_band = lax.all_to_all(grad_band, TENSOR, 0, 0)

    with jax.named_scope("weight_grad"):
        cot8 = got[:, :512]
        top = jnp.max(jnp.abs(cot8), axis=1).astype(F32)
        top = jnp.maximum(top, 1e-30)
        grad = jnp.einsum("tf,jtc->fjc", activations, cot8, preferred_element_type=F32)
        grad = jnp.moveaxis((grad * (LIMIT / top)).astype(F16), 1, 0)
        grad, grad_band = lax.optimization_barrier((grad, grad_band))
        grad = lax.all_to_all(grad, TENSOR, 0, 0)

    with jax.named_scope("pack"):
        low, packed = pl.pallas_call(
            pack_kernel,
            out_shape=[
                jax.ShapeDtypeStruct((8, 64, 128), F32),
                jax.ShapeDtypeStruct((128, 128), F32),
            ],
            compiler_params=params(),
            cost_estimate=cost(100, 1024),
        )(moment_band, grad_band, anchor, table)

    with jax.named_scope("band_total"):
        packed = exchange_sum(packed, ("z", "c"), sizes, (2, 4, 6))
        packed = exchange_sum(packed, ("z", "c"), sizes, (1, 8, 9))
        packed = exchange_sum(packed, ("yh",), sizes, (1,))

    with jax.named_scope("rest"):
        rest = pl.pallas_call(
            rest_kernel,
            grid=(8,),
            in_specs=[
                pl.BlockSpec((1, 64, 128), lambda i: (i, 0, 0)),
                pl.BlockSpec((1024, 128), lambda i: (i, 0)),
                whole(table),
            ],
            out_specs=pl.BlockSpec((1, 1024, 128), lambda i: (i, 0, 0)),
            out_shape=jax.ShapeDtypeStruct((8, 1024, 128), F32),
            compiler_params=params(),
            cost_estimate=cost(3000, 8192),
        )(low, moment0, table)

    with jax.named_scope("input_grad"):
        input_grad = pl.pallas_call(
            input_kernel,
            out_shape=jax.ShapeDtypeStruct((512, 1024), BF16),
            compiler_params=params(),
            cost_estimate=cost(1000, 4096),
        )(got, rows_all)

    with jax.named_scope("weight_step"):
        weight_step = pl.pallas_call(
            step_kernel,
            grid=(8,),
            in_specs=[whole(a) for a in (packed, anchor, table)],
            out_specs=pl.BlockSpec((1024, 128), lambda i: (i, 0)),
            out_shape=jax.ShapeDtypeStruct((8192, 128), BF16),
            scratch_shapes=[pltpu.VMEM((8, 64, 128), F32)],
            compiler_params=params(),
            cost_estimate=cost(3000, 2048),
        )(packed, anchor, table)

    with jax.named_scope("new_momentum"):
        new_momentum = rest + grad.astype(F32) * own_scale

    return (input_grad, new_momentum.reshape(1, 8192, 128), weight_step)


def solution(mesh):
    shape = (2, 8, 2, 4, 2)
    if mesh.devices.size == 16:
        shape = (1, 1, 2, 4, 2)
    names = ("yh", "z", "c", "x", "yl")
    fine = Mesh(mesh.devices.reshape(shape), names)
    dp = ("yh", "z", "c")
    return jax.shard_map(
        functools.partial(body, dict(zip(names, shape))),
        mesh=fine,
        in_specs=(
            P(dp, TENSOR),
            P(dp, TENSOR),
            P(None, TENSOR),
            P(dp, None, TENSOR),
            P(None, TENSOR, None),
        ),
        out_specs=(P(dp, TENSOR), P(dp, None, TENSOR), P(None, TENSOR)),
        check_vma=False,
    )
```

time: 824 us -> 116 us (0.14)
  the two profiles are of different devices: /device:TPU:1 before, /device:TPU:6 now
where the time goes in v1:
time: 116 us; the launch traced here: 115 us
  starting transfers between devices  27 us (23%)
  blocking collectives  20.5 us (18%)
  Pallas kernels  16.2 us (14%)
  local copies, waits for them, and re-layouts  14.6 us (13%)
  between operations  14.2 us (12%)
  waiting for transfers between devices  13 us (11%)
  other arithmetic  5.65 us (5%)
  matrix products  3.89 us (3%)
    all_to_all x1, blocking collectives, body(): got = lax.all_to_all(sent, TENSOR, 0, 0)  20.5 us
    ppermute x7, starting transfers between devices, exchange_sum(): got = [lax.ppermute(v, axes, [(i, i ^ m) for i in range(n)]) for m in moves]  15.1 us
    ppermute x7, waiting for transfers between devices, exchange_sum(): got = [lax.ppermute(v, axes, [(i, i ^ m) for i in range(n)]) for m in moves]  12.3 us
    unnamed x24, local copies, waits for them, and re-layouts  11.2 us
    all_to_all x1, starting transfers between devices, body(): grad = lax.all_to_all(grad, TENSOR, 0, 0)  6.41 us
    all_to_all x1, starting transfers between devices, body(): grad_band = lax.all_to_all(grad_band, TENSOR, 0, 0)  5.43 us
    add x1, other arithmetic, body(): new_momentum = rest + grad.astype(F32) * own_scale  5.31 us
    pallas_call x1, Pallas kernels, body(): pl.pallas_call(step_kernel, grid=(8,), in_specs=[whole(a) for a in (packe...  5.11 us
  transfers between devices with their start and end apart: 10, of which 6 were waited for; matrix products, arithmetic and copies ran while one was open for 10% of the time, Pallas kernels for 12%

profile of v1, /device:TPU:6, one launch (start us, length us, event | category | flops | bytes accessed | tf_op | source)
XLA Modules:
  0.0 115.0 jit_solution(1173330213999043118)
XLA Ops:
  7.2 1.5 %copy-done = bf16[8192,128]{1,0:T(8,128)(2,1)S(1)} copy-done((bf16[8192,128]{1,0:T(8,128)(2,1)S(1)}, bf16[8192,128]{1,0:T(8,128)(2,1)}, u32[]{:S(2)}) %copy-start) | copy-done | bytes 2097176
  8.8 1.0 broadcast_in_dim.2
  9.9 20.5 %all_to_all.15.cot_ref = bf16[8,576,128]{2,1,0:T(8,128)(2,1)S(1)} all-to-all(bf16[8,576,128]{2,1,0:T(8,128)(2,1)S(1)} %pad_maximum_fusion), channel_id=1, replica_groups=mesh['yh'=2,'z'=8,'c'=2,'x'=4,'yl'=2] {'x','yl'}, dimensions={0} | all-to-all | bytes 2359296 | tf_op jit(solution)/shard_map/gather_cotangent/all_to_all | solution.py:242
  32.1 1.2 %copy-done.9 = bf16[512,1024]{1,0:T(8,128)(2,1)S(1)} copy-done((bf16[512,1024]{1,0:T(8,128)(2,1)S(1)}, bf16[512,1024]{1,0:T(8,128)(2,1)}, u32[]{:S(2)}) %copy-start.9) | copy-done | bytes 1048600
  33.3 2.0 %grad_band.1 = f32[8,64,128]{2,1,0:T(8,128)S(1)} custom-call(bf16[512,1024]{1,0:T(8,128)(2,1)S(1)} %copy-done.9, bf16[8,576,128]{2,1,0:T(8,128)(2,1)S(1)} %all_to_all.15.cot_ref, bf16[656,256]{1,0:T(8,128)(2,1)S(1)} %copy-done.3), custom_call_target="tpu_custom_call" | custom-call | flops 2000000000 | bytes 2097152 | tf_op jit(solution)/shard_map/grad_band/pallas_call | solution.py:261
  36.0 5.4 %all-to-all-start.1 = ((f32[8,64,128]{2,1,0:T(8,128)}), f32[8,64,128]{2,1,0:T(8,128)S(1)}, u32[]{:S(2)}, u32[]{:S(2)}) async-start(f32[8,64,128]{2,1,0:T(8,128)} %copy-done.6), calls=%async_computation.1 | async-start | bytes 524288 | tf_op jit(solution)/shard_map/grad_band/all_to_all | solution.py:268
  41.6 3.9 %fusion = f16[8,1024,128]{2,1,0:T(8,128)(2,1)} fusion(f32[8,128]{1,0:T(8,128)S(1)} %maximum_divide_fusion, bf16[512,1024]{1,0:T(8,128)(2,1)} %a_ref.1, bf16[8,576,128]{2,1,0:T(8,128)(2,1)S(1)} %all_to_all.15.cot_ref), kind=kOutput, calls=%fused_computation.2 | convolution fusion | flops 1075838976 | bytes 4198400 | tf_op jit(solution)/shard_map/weight_grad/tf,jtc->fjc/dot_general | solution.py:274
  46.2 6.4 %all-to-all-start.2 = ((f16[8,1024,128]{2,1,0:T(8,128)(2,1)}), f16[8,1024,128]{2,1,0:T(8,128)(2,1)}, u32[]{:S(2)}, u32[]{:S(2)}) async-start(f16[8,1024,128]{2,1,0:T(8,128)(2,1)} %fusion), calls=%async_computation.2 | async-start | bytes 4194304 | tf_op jit(solution)/shard_map/weight_grad/all_to_all | solution.py:277
  55.3 2.2 %copy-done.7 = f32[1,8192,128]{2,1,0:T(8,128)S(1)} copy-done((f32[1,8192,128]{2,1,0:T(8,128)S(1)}, f32[1,8192,128]{2,1,0:T(8,128)}, u32[]{:S(2)}) %copy-start.7) | copy-done | bytes 4194328
  57.5 3.2 %moment_band.1.xm_ref = f32[8,64,128]{2,1,0:T(8,128)S(1)} custom-call(f32[8192,128]{1,0:T(8,128)S(1)} %bitcast.11, bf16[656,256]{1,0:T(8,128)(2,1)S(1)} %copy-done.4), custom_call_target="tpu_custom_call" | custom-call | flops 2000000000 | bytes 4194304 | tf_op jit(solution)/shard_map/moment_band/pallas_call | solution.py:248
  61.1 3.4 %collective-permute-start.1 = (f32[128,128]{1,0:T(8,128)S(1)}, f32[128,128]{1,0:T(8,128)S(1)}, u32[]{:S(2)}, u32[]{:S(2)}) collective-permute-start(f32[128,128]{1,0:T(8,128)S(1)} %get-tuple-element.14), channel_id=1, source_target_pairs={{0,32},{8,40},{16,48},{24,56},{32,0},{40,8},{48,16},{56,24},{64,96... | collective-permute-start | bytes 196616 | tf_op jit(solution)/shard_map/band_total/ppermute | solution.py:225
  64.5 1.5 %collective-permute-start.2 = (f32[128,128]{1,0:T(8,128)S(1)}, f32[128,128]{1,0:T(8,128)S(1)}, u32[]{:S(2)}, u32[]{:S(2)}) collective-permute-start(f32[128,128]{1,0:T(8,128)S(1)} %get-tuple-element.14), channel_id=1, source_target_pairs={{0,48},{8,56},{16,32},{24,40},{32,16},{40,24},{48,0},{56,8},{64,11... | collective-permute-start | bytes 196616 | tf_op jit(solution)/shard_map/band_total/ppermute | solution.py:225
  66.5 3.1 %collective-permute-done.1 = f32[128,128]{1,0:T(8,128)S(1)} collective-permute-done((f32[128,128]{1,0:T(8,128)S(1)}, f32[128,128]{1,0:T(8,128)S(1)}, u32[]{:S(2)}, u32[]{:S(2)}) %collective-permute-start.1) | collective-permute-done | bytes 65568 | tf_op jit(solution)/shard_map/band_total/ppermute | solution.py:225
  69.6 1.1 collective-permute-done.2
  71.2 5.9 %collective-permute-start.4 = (f32[128,128]{1,0:T(8,128)S(1)}, f32[128,128]{1,0:T(8,128)S(1)}, u32[]{:S(2)}, u32[]{:S(2)}) collective-permute-start(f32[128,128]{1,0:T(8,128)S(1)} %add_add_fusion.1), channel_id=1, source_target_pairs={{0,64},{8,72},{16,80},{24,88},{32,96},{40,104},{48,112},{56,120},{... | collective-permute-start | bytes 196616 | tf_op jit(solution)/shard_map/band_total/ppermute | solution.py:225
  77.4 2.2 %collective-permute-done.4 = f32[128,128]{1,0:T(8,128)S(1)} collective-permute-done((f32[128,128]{1,0:T(8,128)S(1)}, f32[128,128]{1,0:T(8,128)S(1)}, u32[]{:S(2)}, u32[]{:S(2)}) %collective-permute-start.4) | collective-permute-done | bytes 65568 | tf_op jit(solution)/shard_map/band_total/ppermute | solution.py:225
  79.6 5.3 %collective-permute-done.5 = f32[128,128]{1,0:T(8,128)S(1)} collective-permute-done((f32[128,128]{1,0:T(8,128)S(1)}, f32[128,128]{1,0:T(8,128)S(1)}, u32[]{:S(2)}, u32[]{:S(2)}) %collective-permute-start.5) | collective-permute-done | bytes 65568 | tf_op jit(solution)/shard_map/band_total/ppermute | solution.py:225
  84.9 3.7 %collective-permute-start.6 = (f32[128,128]{1,0:T(8,128)S(1)}, f32[128,128]{1,0:T(8,128)S(1)}, u32[]{:S(2)}, u32[]{:S(2)}) collective-permute-start(f32[128,128]{1,0:T(8,128)S(1)} %add_add_fusion), channel_id=1, source_target_pairs={{0,128},{128,0},{1,129},{129,1},{2,130},{130,2},{3,131},{131,3},{4... | collective-permute-start | bytes 196616 | tf_op jit(solution)/shard_map/band_total/ppermute | solution.py:225
  88.6 3.3 %rest.1 = f32[8,1024,128]{2,1,0:T(8,128)S(1)} custom-call(f32[8,64,128]{2,1,0:T(8,128)S(1)} %get-tuple-element.12.low_ref, f32[8192,128]{1,0:T(8,128)S(1)} %bitcast.12, bf16[656,256]{1,0:T(8,128)(2,1)S(1)} %copy-done.5), custom_call_target="tpu_custom_call" | custom-call | flops 3000000000 | bytes 8388608 | tf_op jit(solution)/shard_map/rest/pallas_call | solution.py:296
  91.9 2.0 %copy-done.1 = f32[8,1024,128]{2,1,0:T(8,128)} copy-done((f32[8,1024,128]{2,1,0:T(8,128)}, f32[8,1024,128]{2,1,0:T(8,128)S(1)}, u32[]{:S(2)}) %copy-start.1) | copy-done | bytes 4194328
  93.9 5.1 %weight_step.1 = bf16[8192,128]{1,0:T(8,128)(2,1)} custom-call(f32[128,128]{1,0:T(8,128)S(1)} %add.39.pack_ref, bf16[32,16]{1,0:T(8,128)(2,1)S(1)} %convert_element_type.33.a_ref, bf16[656,256]{1,0:T(8,128)(2,1)S(1)} %copy-done.5), custom_call_target="tpu_custom_call" | custom-call | flops 3000000000 | bytes 2097152 | tf_op jit(solution)/shard_map/weight_step/pallas_call | solution.py:319
  99.0 5.3 %multiply_add_fusion = f32[8,1024,128]{2,1,0:T(8,128)} fusion(f32[8,1024,128]{2,1,0:T(8,128)} %copy-done.1, f16[8,1024,128]{2,1,0:T(8,128)(2,1)} %all-to-all-done.2, f32[128]{0:T(128)S(1)} %maximum_multiply_fusion), kind=kLoop, calls=%fused_computation | loop fusion | flops 3145728 | bytes 10486272 | tf_op jit(solution)/shard_map/new_momentum/add | solution.py:331
  104.3 1.6 %copy-done.2 = bf16[128,64,128]{2,1,0:T(8,128)(2,1)S(1)} copy-done((bf16[128,64,128]{2,1,0:T(8,128)(2,1)S(1)}, bf16[128,64,128]{2,1,0:T(8,128)(2,1)}, u32[]{:S(2)}) %copy-start.2) | copy-done | bytes 2097176
  105.9 2.3 %input_grad.1 = bf16[512,1024]{1,0:T(8,128)(2,1)} custom-call(bf16[8,576,128]{2,1,0:T(8,128)(2,1)S(1)} %all_to_all.15.cot_ref, bf16[16,8,64,128]{3,2,1,0:T(8,128)(2,1)S(1)} %bitcast.10), custom_call_target="tpu_custom_call" | custom-call | flops 1000000000 | bytes 4194304 | tf_op jit(solution)/shard_map/input_grad/pallas_call | solution.py:311
  (44 shorter events, 7.7 us)
Async XLA Ops:
  7.2 1.6 %copy-start = (bf16[8192,128]{1,0:T(8,128)(2,1)S(1)}, bf16[8192,128]{1,0:T(8,128)(2,1)}, u32[]{:S(2)}) copy-start(bf16[8192,128]{1,0:T(8,128)(2,1)} %param.8) | copy-start | bytes 6291460
  7.2 97.1 %all-gather.3.cloned.1.call-start = ((), (), s32[]{:S(2)}) async-start(), calls=%async_computation.3 | async-start | bytes 2228224 | tf_op jit(solution)/shard_map/share_weight/all_gather | solution.py:245
  31.1 1.0 copy-start.3
  32.0 1.2 %copy-start.9 = (bf16[512,1024]{1,0:T(8,128)(2,1)S(1)}, bf16[512,1024]{1,0:T(8,128)(2,1)}, u32[]{:S(2)}) copy-start(bf16[512,1024]{1,0:T(8,128)(2,1)} %a_ref.1) | copy-start | bytes 3145732
  35.3 0.7 copy-start.6
  36.0 10.2 %all-to-all-start.1 = ((f32[8,64,128]{2,1,0:T(8,128)}), f32[8,64,128]{2,1,0:T(8,128)S(1)}, u32[]{:S(2)}, u32[]{:S(2)}) async-start(f32[8,64,128]{2,1,0:T(8,128)} %copy-done.6), calls=%async_computation.1 | async-start | bytes 524288 | tf_op jit(solution)/shard_map/grad_band/all_to_all | solution.py:268
  45.5 7.1 %copy-start.11 = (s32[128,2,2]{0,2,1:T(2,128)S(1)}, s32[128,2,2]{0,2,1:T(2,128)}, u32[]{:S(2)}) copy-start(s32[128,2,2]{0,2,1:T(2,128)} %param.10) | copy-start | bytes 6148
  46.2 52.8 %all-to-all-start.2 = ((f16[8,1024,128]{2,1,0:T(8,128)(2,1)}), f16[8,1024,128]{2,1,0:T(8,128)(2,1)}, u32[]{:S(2)}, u32[]{:S(2)}) async-start(f16[8,1024,128]{2,1,0:T(8,128)(2,1)} %fusion), calls=%async_computation.2 | async-start | bytes 4194304 | tf_op jit(solution)/shard_map/weight_grad/all_to_all | solution.py:277
  54.4 1.0 copy-start.4
  55.3 2.2 %copy-start.7 = (f32[1,8192,128]{2,1,0:T(8,128)S(1)}, f32[1,8192,128]{2,1,0:T(8,128)}, u32[]{:S(2)}) copy-start(f32[1,8192,128]{2,1,0:T(8,128)} %param.9) | copy-start | bytes 12582916
  57.5 8.9 %copy-start.10 = (bf16[512,128]{1,0:T(8,128)(2,1)S(1)}, bf16[512,128]{1,0:T(8,128)(2,1)}, u32[]{:S(2)}) copy-start(bf16[512,128]{1,0:T(8,128)(2,1)} %param.7) | copy-start | bytes 393220
  57.5 31.1 %copy-start.5 = (bf16[656,256]{1,0:T(8,128)(2,1)S(1)}, bf16[656,256]{1,0:T(8,128)(2,1)}, u32[]{:S(2)}) copy-start(bf16[656,256]{1,0:T(8,128)(2,1)} %constant.31.clone.table_ref) | copy-start | bytes 1007620
  57.5 31.1 %copy-start.8 = (f32[1,8192,128]{2,1,0:T(8,128)S(1)}, f32[1,8192,128]{2,1,0:T(8,128)}, u32[]{:S(2)}) copy-start(f32[1,8192,128]{2,1,0:T(8,128)} %param.9) | copy-start | bytes 12582916
  61.1 8.5 %collective-permute-start.1 = (f32[128,128]{1,0:T(8,128)S(1)}, f32[128,128]{1,0:T(8,128)S(1)}, u32[]{:S(2)}, u32[]{:S(2)}) collective-permute-start(f32[128,128]{1,0:T(8,128)S(1)} %get-tuple-element.14), channel_id=1, source_target_pairs={{0,32},{8,40},{16,48},{24,56},{32,0},{40,8},{48,16},{56,24},{64,96... | collective-permute-start | bytes 196616 | tf_op jit(solution)/shard_map/band_total/ppermute | solution.py:225
  64.5 6.2 %collective-permute-start.2 = (f32[128,128]{1,0:T(8,128)S(1)}, f32[128,128]{1,0:T(8,128)S(1)}, u32[]{:S(2)}, u32[]{:S(2)}) collective-permute-start(f32[128,128]{1,0:T(8,128)S(1)} %get-tuple-element.14), channel_id=1, source_target_pairs={{0,48},{8,56},{16,32},{24,40},{32,16},{40,24},{48,0},{56,8},{64,11... | collective-permute-start | bytes 196616 | tf_op jit(solution)/shard_map/band_total/ppermute | solution.py:225
  66.0 5.2 %collective-permute-start = (f32[128,128]{1,0:T(8,128)S(1)}, f32[128,128]{1,0:T(8,128)S(1)}, u32[]{:S(2)}, u32[]{:S(2)}) collective-permute-start(f32[128,128]{1,0:T(8,128)S(1)} %get-tuple-element.14), channel_id=1, source_target_pairs={{0,16},{8,24},{16,0},{24,8},{32,48},{40,56},{48,32},{56,40},{64,80... | collective-permute-start | bytes 196616 | tf_op jit(solution)/shard_map/band_total/ppermute | solution.py:225
  71.2 8.4 %collective-permute-start.4 = (f32[128,128]{1,0:T(8,128)S(1)}, f32[128,128]{1,0:T(8,128)S(1)}, u32[]{:S(2)}, u32[]{:S(2)}) collective-permute-start(f32[128,128]{1,0:T(8,128)S(1)} %add_add_fusion.1), channel_id=1, source_target_pairs={{0,64},{8,72},{16,80},{24,88},{32,96},{40,104},{48,112},{56,120},{... | collective-permute-start | bytes 196616 | tf_op jit(solution)/shard_map/band_total/ppermute | solution.py:225
  77.1 7.8 %collective-permute-start.5 = (f32[128,128]{1,0:T(8,128)S(1)}, f32[128,128]{1,0:T(8,128)S(1)}, u32[]{:S(2)}, u32[]{:S(2)}) collective-permute-start(f32[128,128]{1,0:T(8,128)S(1)} %add_add_fusion.1), channel_id=1, source_target_pairs={{0,72},{8,64},{16,88},{24,80},{32,104},{40,96},{48,120},{56,112},{... | collective-permute-start | bytes 196616 | tf_op jit(solution)/shard_map/band_total/ppermute | solution.py:225
  77.1 7.8 %collective-permute-start.3 = (f32[128,128]{1,0:T(8,128)S(1)}, f32[128,128]{1,0:T(8,128)S(1)}, u32[]{:S(2)}, u32[]{:S(2)}) collective-permute-start(f32[128,128]{1,0:T(8,128)S(1)} %add_add_fusion.1), channel_id=1, source_target_pairs={{0,8},{8,0},{16,24},{24,16},{32,40},{40,32},{48,56},{56,48},{64,72... | collective-permute-start | bytes 196616 | tf_op jit(solution)/shard_map/band_total/ppermute | solution.py:225
  84.9 8.9 %collective-permute-start.6 = (f32[128,128]{1,0:T(8,128)S(1)}, f32[128,128]{1,0:T(8,128)S(1)}, u32[]{:S(2)}, u32[]{:S(2)}) collective-permute-start(f32[128,128]{1,0:T(8,128)S(1)} %add_add_fusion), channel_id=1, source_target_pairs={{0,128},{128,0},{1,129},{129,1},{2,130},{130,2},{3,131},{131,3},{4... | collective-permute-start | bytes 196616 | tf_op jit(solution)/shard_map/band_total/ppermute | solution.py:225
  91.9 2.0 %copy-start.1 = (f32[8,1024,128]{2,1,0:T(8,128)}, f32[8,1024,128]{2,1,0:T(8,128)S(1)}, u32[]{:S(2)}) copy-start(f32[8,1024,128]{2,1,0:T(8,128)S(1)} %rest.1) | copy-start | bytes 12582916
  104.3 1.6 %copy-start.2 = (bf16[128,64,128]{2,1,0:T(8,128)(2,1)S(1)}, bf16[128,64,128]{2,1,0:T(8,128)(2,1)}, u32[]{:S(2)}) copy-start(bf16[128,64,128]{2,1,0:T(8,128)(2,1)} %all-gather.3.cloned.1.call-done) | copy-start | bytes 6291460
Sparse Core Ops, SparseCore 0:
  31.2 42.5 all-gather.2

commit v2 on v1

v2 whole, which is shorter than its diff:
```python
import functools

import jax
import jax.numpy as jnp
import numpy as np
from jax import lax
from jax.experimental import pallas as pl
from jax.experimental.pallas import tpu as pltpu
from jax.sharding import Mesh
from jax.sharding import PartitionSpec as P

GROUP = 64
BAND = 8
FREQ = 16
DECAY = 0.9
LIMIT = 20.0

F32, BF16, F16 = jnp.float32, jnp.bfloat16, jnp.float16
TENSOR = ("x", "yl")
NT = (((1,), (1,)), ((), ()))


def split_const(a):
    a = np.asarray(a, np.float32)
    hi = a.astype(jnp.bfloat16)
    lo = (a - hi.astype(np.float32)).astype(jnp.bfloat16)
    return hi, lo


def tables():
    f = np.arange(FREQ)[:, None]
    a = np.arange(GROUP)[None, :]
    scale = np.where(f == 0, np.sqrt(1 / GROUP), np.sqrt(2 / GROUP))
    c16 = scale * np.cos(np.pi * (2 * a + 1) * f / (2 * GROUP))
    rows = np.kron(np.eye(4), c16)
    cols = np.tile(np.kron(np.eye(2), c16.T), (1, 4))
    rh, rl = split_const(rows)
    th, tl = split_const(rows.T)
    ch, cl = split_const(cols)
    uh, ul = split_const(cols.T)
    return np.concatenate(
        [
            rh,
            rl,
            np.concatenate([th, tl, th, np.zeros_like(th)], axis=1),
            np.concatenate([ch, cl], axis=1),
            np.concatenate([uh, ul], axis=1),
        ],
        axis=0,
    )


ROWS = slice(0, 128)
ROWS_T = slice(128, 384)
COLS = slice(384, 512)
COLS_T = slice(512, 640)


def split(a):
    hi = a.astype(BF16)
    return hi, (a - hi.astype(F32)).astype(BF16)


def mm(a, b):
    return jnp.dot(a, b, preferred_element_type=F32)


def times_table(a, table):
    hi, lo = split(a)
    both = mm(hi, table)
    return both[:, :128] + (both[:, 128:] + mm(lo, table[:, :128]))


def lane_block(shape, kk):
    lane = lax.broadcasted_iota(jnp.int32, shape, len(shape) - 1)
    return lane // 32 == kk


def pick_lanes(parts):
    out = parts[0]
    for kk in range(1, 4):
        out = jnp.where(lane_block(out.shape, kk), parts[kk], out)
    return out


def anchor_lanes(anchor_ref):
    row = lax.broadcasted_iota(jnp.int32, (32, 128), 0)
    group = lax.broadcasted_iota(jnp.int32, (32, 128), 1)
    own = group // 4 == row
    group = lax.broadcasted_iota(jnp.int32, (128, 128), 0)
    lane = lax.broadcasted_iota(jnp.int32, (128, 128), 1)
    out = []
    for which in range(2):
        v = jnp.zeros((32, 128), F32)
        for l in range(2):
            at = jnp.where(own, anchor_ref[l, which : which + 1, :].astype(F32), 0.0)
            to = (group % 4 == lane // 32) & (lane // FREQ % 2 == l)
            v += mm(at.astype(BF16), jnp.where(to, 1.0, 0.0).astype(BF16))
        out.append(v)
    return out


def band_mask(r, c):
    f = lax.broadcasted_iota(jnp.int32, (FREQ, 128), 0).astype(F32)
    g = (lax.broadcasted_iota(jnp.int32, (FREQ, 128), 1) % FREQ).astype(F32)
    out = []
    for q in range(4):
        rq, cq = r[q : q + 1, :], c[q : q + 1, :]
        inside = (f >= rq) & (f < rq + BAND) & (g >= cq) & (g < cq + BAND)
        out.append(jnp.where(inside, 1.0, 0.0))
    return jnp.concatenate(out, axis=0)


def row_bands(m, table_ref, z_ref, t):
    for q in range(4):
        both = jnp.concatenate(split(m[q * 256 : (q + 1) * 256, :]), axis=1)
        v = mm(table_ref[ROWS, :], both)
        z_ref[t, q * 64 : (q + 1) * 64, :] = v[:64, :128] + (v[:64, 128:] + v[64:, :128])


def column_bands(table_ref, z_ref, low_ref, r, c):
    for t in range(8):
        y = times_table(z_ref[t], table_ref[COLS, :])
        for q in range(4):
            low_ref[t, q * 16 : (q + 1) * 16, :] = pick_lanes(
                [y[q * 64 + kk * 16 : q * 64 + (kk + 1) * 16] for kk in range(4)]
            )
        low_ref[t] = low_ref[t] * band_mask(r[4 * t : 4 * t + 4], c[4 * t : 4 * t + 4])


def moment_band_kernel(m_hbm, a_hbm, anchor_ref, table_ref, low_ref, act_ref, *scratch):
    m_ref, a_ref, z_ref, sems = scratch
    get_m = [
        pltpu.make_async_copy(m_hbm.at[pl.ds(t * 1024, 1024)], m_ref.at[t], sems.at[t])
        for t in range(8)
    ]
    get_a = pltpu.make_async_copy(a_hbm, a_ref, sems.at[8])
    get_a.start()
    for copy in get_m:
        copy.start()
    r, c = anchor_lanes(anchor_ref)
    get_a.wait()
    for q in range(4):
        v = lax.dot_general(
            table_ref[ROWS, :], a_ref[:, q * 256 : (q + 1) * 256], NT, preferred_element_type=F32
        )
        rows = slice(q * 64, (q + 1) * 64)
        act_ref[0, rows, :], act_ref[1, rows, :] = split(v[:64] + v[64:])
    for t in range(8):
        get_m[t].wait()
        row_bands(m_ref.at[t], table_ref, z_ref, t)
    column_bands(table_ref, z_ref, low_ref, r, c)
    low_ref[...] = DECAY * low_ref[...]


def send_kernel(cot_hbm, w_hbm, o_hbm, cot_ref, w_ref, sems):
    part = w_ref.shape[1]
    at = pl.multiple_of(share_index(part) * part, part)
    get_w = pltpu.make_async_copy(w_hbm.at[:, pl.ds(at, part)], w_ref, sems.at[0])
    get_cot = pltpu.make_async_copy(cot_hbm, cot_ref, sems.at[1])
    put_w = pltpu.make_async_copy(w_ref, o_hbm.at[:, pl.ds(512, part)], sems.at[2])
    put_cot = [
        pltpu.make_async_copy(cot_ref, o_hbm.at[j, pl.ds(0, 512)], sems.at[3 + j])
        for j in range(8)
    ]
    get_cot.start()
    get_w.start()
    get_cot.wait()
    for copy in put_cot:
        copy.start()
    get_w.wait()
    put_w.start()
    for copy in put_cot:
        copy.wait()
    put_w.wait()


def share_index(part, core=0, z=0):
    pairs = 1024 // (part * lax.axis_size("c"))
    mine = jnp.bitwise_xor(lax.axis_index("c"), core) * pairs
    if pairs > 1:
        mine = mine + jnp.bitwise_xor(lax.rem(lax.axis_index("z"), 2), z)
    return mine


def grad_band_kernel(act_hbm, cot_ref, table_hbm, o_hbm, *scratch):
    act_ref, table_ref, out, sems = scratch
    get_table = pltpu.make_async_copy(table_hbm.at[COLS], table_ref, sems.at[0])
    get_act = pltpu.make_async_copy(act_hbm, act_ref, sems.at[1])
    put = []
    for copy in (get_table, get_act):
        copy.start()
    get_table.wait()
    get_act.wait()
    high, low = act_ref[0], act_ref[1]
    for j in range(0, 8, 2):
        halves = []
        for i in range(2):
            both = mm(cot_ref[j + i, :512, :], table_ref[...])
            halves.append(split(both[:, :128] + both[:, 128:]))
        rh = jnp.concatenate([halves[0][0], halves[1][0]], axis=1)
        rl = jnp.concatenate([halves[0][1], halves[1][1]], axis=1)
        x = mm(high, rh) + (mm(high, rl) + mm(low, rh))
        for i in range(2):
            for q in range(4):
                out[j + i, q * 16 : (q + 1) * 16, :] = pick_lanes(
                    [
                        x[q * 64 + kk * 16 : q * 64 + (kk + 1) * 16, i * 128 : (i + 1) * 128]
                        for kk in range(4)
                    ]
                )
        two = pl.ds(j, 2)
        put.append(pltpu.make_async_copy(out.at[two], o_hbm.at[two], sems.at[5 + j // 2]))
        put[-1].start()
    for copy in put:
        copy.wait()


def pack_kernel(moment_hbm, grad_ref, anchor_ref, low_ref, keep_ref, give_ref, *scratch):
    moment_ref, pack_ref, sem = scratch
    get = pltpu.make_async_copy(moment_hbm, moment_ref, sem)
    get.start()
    r, c = anchor_lanes(anchor_ref)
    get.wait()
    for t in range(8):
        mask = band_mask(r[4 * t : 4 * t + 4], c[4 * t : 4 * t + 4])
        low_ref[t] = mask * grad_ref[t] + moment_ref[t]
    rows = low_ref[...].reshape(8, 4, 2, 8, 128)
    rows = (rows[:, :, 0] + rows[:, :, 1]).reshape(2, 128, 128)
    a, b = rows[0], rows[1]
    lane = lax.broadcasted_iota(jnp.int32, a.shape, 1)
    pack_ref[...] = jnp.where(lane % 16 < 8, a + pltpu.roll(a, 120, 1), b + pltpu.roll(b, 8, 1))
    core = lax.axis_index("c")
    keep_ref[...] = pack_ref[core_rows(core), :]
    give_ref[...] = pack_ref[core_rows(1 - core), :]


def core_rows(core):
    return pl.ds(pl.multiple_of(core * 64, 64), 64)


def unpack(p):
    low = lax.broadcasted_iota(jnp.int32, p.shape, 1) % 16 < 8
    a = jnp.where(low, p, pltpu.roll(p, 8, 1))
    b = jnp.where(low, pltpu.roll(p, 120, 1), p)
    r = jnp.concatenate([a, b], axis=0).reshape(8, 4, 1, 8, 128)
    return jnp.broadcast_to(r, (8, 4, 2, 8, 128)).reshape(8, 64, 128)


def rebuild(low_ref, table_ref, v_ref, emit):
    for t in range(8):
        spread = []
        for q in range(4):
            part = low_ref[t, q * 16 : (q + 1) * 16, :]
            spread += [jnp.where(lane_block(part.shape, kk), part, 0.0) for kk in range(4)]
        v = times_table(jnp.concatenate(spread, axis=0), table_ref[COLS_T, :])
        for n in range(2):
            rows = [v[(2 * n + i) * 64 : (2 * n + i + 1) * 64] for i in range(2)]
            hi, lo = split(jnp.concatenate(rows, axis=1))
            v_ref[t, n] = jnp.concatenate([hi, hi, lo], axis=0)
    for t in range(8):
        for n in range(2):
            both = mm(table_ref[ROWS_T, :192], v_ref[t, n])
            emit(t, 2 * n, both[:, :128])
            emit(t, 2 * n + 1, both[:, 128:])


def rest_kernel(low_ref, m_hbm, table_hbm, o_hbm, table_ref, m_ref, v_ref, sems):
    get_table = pltpu.make_async_copy(table_hbm, table_ref, sems.at[1])
    get_m = [
        pltpu.make_async_copy(m_hbm.at[pl.ds(t * 1024, 1024)], m_ref.at[t], sems.at[2 + t])
        for t in range(8)
    ]
    put = [pltpu.make_async_copy(m_ref.at[t], o_hbm.at[t], sems.at[10 + t]) for t in range(8)]
    for copy in [get_table] + get_m:
        copy.start()
    get_table.wait()

    def emit(t, q, v):
        if q == 0:
            get_m[t].wait()
        rows = slice(q * 256, (q + 1) * 256)
        m_ref[t, rows, :] = DECAY * m_ref[t, rows, :] - v
        if q == 3:
            put[t].start()

    rebuild(low_ref, table_ref, v_ref, emit)
    for copy in put:
        copy.wait()


def step_kernel(mine_ref, other_ref, anchor_ref, table_hbm, o_hbm, *scratch):
    low_ref, pack_ref, table_ref, v_ref, o_ref, sems = scratch
    get_table = pltpu.make_async_copy(table_hbm, table_ref, sems.at[8])
    put = [
        pltpu.make_async_copy(o_ref.at[t], o_hbm.at[pl.ds(t * 1024, 1024)], sems.at[t])
        for t in range(8)
    ]
    get_table.start()
    core = lax.axis_index("c")
    pack_ref[core_rows(core), :] = mine_ref[...]
    pack_ref[core_rows(1 - core), :] = other_ref[...]
    r, c = anchor_lanes(anchor_ref)
    low_ref[...] = unpack(pack_ref[...])
    for t in range(8):
        low_ref[t] = low_ref[t] * band_mask(r[4 * t : 4 * t + 4], c[4 * t : 4 * t + 4])
    get_table.wait()

    def emit(t, q, v):
        o_ref[t, q * 256 : (q + 1) * 256, :] = v.astype(BF16)
        if q == 3:
            put[t].start()

    rebuild(low_ref, table_ref, v_ref, emit)
    for copy in put:
        copy.wait()


def input_kernel(cot_hbm, *refs):
    count = len(refs) - 5
    w_hbm, o_hbm = refs[:count], refs[count]
    cot_ref, w_ref, o_ref, sems = refs[count + 1 :]
    part = w_ref.shape[2]
    get_cot = [
        pltpu.make_async_copy(
            cot_hbm.at[j, pl.ds(0, 512)], cot_ref.at[:, pl.ds(j * 128, 128)], sems.at[j]
        )
        for j in range(8)
    ]
    get_w = [pltpu.make_async_copy(w_hbm[n], w_ref.at[n], sems.at[8 + n]) for n in range(count)]
    for copy in get_cot + get_w:
        copy.start()
    put = []
    for copy in get_cot:
        copy.wait()
    for n in range(count):
        get_w[n].wait()
        rhs = jnp.concatenate([w_ref[n, j] for j in range(8)], axis=1)
        v = lax.dot_general(cot_ref[...], rhs, NT, preferred_element_type=F32)
        o_ref[n] = v.astype(BF16)
        share = share_index(part, n % 2, n // 2)
        lanes = pl.ds(pl.multiple_of(share * part, part), part)
        put.append(pltpu.make_async_copy(o_ref.at[n], o_hbm.at[:, lanes], sems.at[12 + n]))
        put[-1].start()
    for copy in put:
        copy.wait()


HBM = pl.BlockSpec(memory_space=pltpu.HBM)
VMEM = pl.BlockSpec(memory_space=pltpu.VMEM)


def whole(a):
    return pl.BlockSpec(a.shape, lambda i: (0,) * a.ndim)


def params(mib=16):
    return pltpu.CompilerParams(vmem_limit_bytes=mib * 2**20)


def cost(mflops, kib):
    return pl.CostEstimate(
        flops=mflops * 10**6, bytes_accessed=kib * 2**10, transcendentals=0
    )


def exchange_sum(v, axes, sizes, move):
    n = int(np.prod([sizes[a] for a in axes]))
    if move >= n:
        return v
    return v + lax.ppermute(v, axes, [(i, i ^ move) for i in range(n)])


def body(sizes, activations, cotangent, weight, momentum, band_anchor):
    table = jnp.asarray(tables())
    nz, nc = sizes["z"], sizes["c"]
    moment0 = momentum[0]
    anchor = band_anchor.transpose(1, 2, 0)

    pairs = 2 if nz > 1 else 1
    part = 1024 // (pairs * nc)
    with jax.named_scope("gather_cotangent"):
        sent = pl.pallas_call(
            send_kernel,
            in_specs=[HBM] * 2,
            out_specs=HBM,
            out_shape=jax.ShapeDtypeStruct((8, 512 + part, 128), BF16),
            scratch_shapes=[
                pltpu.VMEM((512, 128), BF16),
                pltpu.VMEM((8, part, 128), BF16),
                pltpu.SemaphoreType.DMA((11,)),
            ],
            compiler_params=params(56),
            cost_estimate=cost(1, 2048),
        )(cotangent, weight.reshape(8, 1024, 128))
        got = lax.all_to_all(sent, TENSOR, 0, 0)

    with jax.named_scope("moment_band"):
        moment_band, act_band = pl.pallas_call(
            moment_band_kernel,
            in_specs=[HBM, HBM, VMEM, VMEM],
            out_specs=[VMEM] * 2,
            out_shape=[
                jax.ShapeDtypeStruct((8, 64, 128), F32),
                jax.ShapeDtypeStruct((2, 256, 512), BF16),
            ],
            scratch_shapes=[
                pltpu.VMEM((8, 1024, 128), F32),
                pltpu.VMEM((512, 1024), BF16),
                pltpu.VMEM((8, 256, 128), F32),
                pltpu.SemaphoreType.DMA((9,)),
            ],
            compiler_params=params(52),
            cost_estimate=cost(2000, 5120),
        )(moment0, activations, anchor, table)
        got, moment_band, act_band = lax.optimization_barrier((got, moment_band, act_band))

    own_scale = jnp.maximum(jnp.max(jnp.abs(cotangent), axis=0).astype(F32), 1e-30) / LIMIT

    swap = [(i, nc - 1 - i) for i in range(nc)]
    with jax.named_scope("weight_share"):
        share = got[:, 512:]
        shares = [share, lax.ppermute(share, "c", swap)]
        if pairs > 1:
            share = lax.ppermute(share, "z", [(k, k ^ 1) for k in range(nz)])
            shares += [share, lax.ppermute(share, "c", swap)]

    with jax.named_scope("grad_band"):
        grad_band = pl.pallas_call(
            grad_band_kernel,
            in_specs=[HBM, VMEM, HBM],
            out_specs=HBM,
            out_shape=jax.ShapeDtypeStruct((8, 64, 128), F32),
            scratch_shapes=[
                pltpu.VMEM((2, 256, 512), BF16),
                pltpu.VMEM((128, 256), BF16),
                pltpu.VMEM((8, 64, 128), F32),
                pltpu.SemaphoreType.DMA((9,)),
            ],
            compiler_params=params(40),
            cost_estimate=cost(2000, 2048),
        )(act_band, got, table)
        got, grad_band = lax.optimization_barrier((got, grad_band))
        grad_band = lax.all_to_all(grad_band, TENSOR, 0, 0)

    with jax.named_scope("weight_grad"):
        cot8 = got[:, :512]
        top = jnp.max(jnp.abs(cot8), axis=1).astype(F32)
        top = jnp.maximum(top, 1e-30)
        grad = jnp.einsum("tf,jtc->fjc", activations, cot8, preferred_element_type=F32)
        grad = jnp.moveaxis((grad * (LIMIT / top)).astype(F16), 1, 0)
        grad, grad_band, shares = lax.optimization_barrier((grad, grad_band, shares))
        grad = lax.all_to_all(grad, TENSOR, 0, 0)

    with jax.named_scope("pack"):
        low, mine, other = pl.pallas_call(
            pack_kernel,
            in_specs=[HBM, VMEM, VMEM],
            out_specs=[VMEM] * 3,
            out_shape=[jax.ShapeDtypeStruct((8, 64, 128), F32)]
            + [jax.ShapeDtypeStruct((64, 128), F32)] * 2,
            scratch_shapes=[
                pltpu.VMEM((8, 64, 128), F32),
                pltpu.VMEM((128, 128), F32),
                pltpu.SemaphoreType.DMA,
            ],
            compiler_params=params(),
            cost_estimate=cost(100, 1024),
        )(moment_band, grad_band, anchor)

    with jax.named_scope("rest"):
        rest = pl.pallas_call(
            rest_kernel,
            in_specs=[VMEM, HBM, HBM],
            out_specs=HBM,
            out_shape=jax.ShapeDtypeStruct((8, 1024, 128), F32),
            scratch_shapes=[
                pltpu.VMEM(table.shape, BF16),
                pltpu.VMEM((8, 1024, 128), F32),
                pltpu.VMEM((8, 2, 192, 256), BF16),
                pltpu.SemaphoreType.DMA((18,)),
            ],
            compiler_params=params(56),
            cost_estimate=cost(3000, 8192),
        )(low, moment0, table)

    with jax.named_scope("input_grad"):
        input_grad = pl.pallas_call(
            input_kernel,
            in_specs=[HBM] * (1 + len(shares)),
            out_specs=HBM,
            out_shape=jax.ShapeDtypeStruct((512, 1024), BF16),
            scratch_shapes=[
                pltpu.VMEM((512, 1024), BF16),
                pltpu.VMEM((len(shares), 8, part, 128), BF16),
                pltpu.VMEM((len(shares), 512, part), BF16),
                pltpu.SemaphoreType.DMA((16,)),
            ],
            compiler_params=params(16),
            cost_estimate=cost(1000, 4096),
        )(got, *shares)

    with jax.named_scope("band_total"):
        mine = mine + lax.ppermute(other, "c", swap)
        mine = exchange_sum(mine, ("z",), sizes, 1)
        mine, rest = lax.optimization_barrier((mine, rest))
        mine = exchange_sum(mine, ("z",), sizes, 3)
        mine, input_grad = lax.optimization_barrier((mine, input_grad))
        mine = exchange_sum(mine, ("z",), sizes, 7)
        mine = exchange_sum(mine, ("yh",), sizes, 1)

    with jax.named_scope("new_momentum"):
        other = lax.ppermute(mine, "c", swap)
        new_momentum = rest + grad.astype(F32) * own_scale

    with jax.named_scope("weight_step"):
        weight_step = pl.pallas_call(
            step_kernel,
            in_specs=[VMEM] * 3 + [HBM],
            out_specs=HBM,
            out_shape=jax.ShapeDtypeStruct((8192, 128), BF16),
            scratch_shapes=[
                pltpu.VMEM((8, 64, 128), F32),
                pltpu.VMEM((128, 128), F32),
                pltpu.VMEM(table.shape, BF16),
                pltpu.VMEM((8, 2, 192, 256), BF16),
                pltpu.VMEM((8, 1024, 128), BF16),
                pltpu.SemaphoreType.DMA((10,)),
            ],
            compiler_params=params(16),
            cost_estimate=cost(3000, 2048),
        )(mine, other, anchor, table)

    return (input_grad, new_momentum.reshape(1, 8192, 128), weight_step)


def solution(mesh):
    shape = (2, 8, 2, 4, 2)
    if mesh.devices.size == 16:
        shape = (1, 1, 2, 4, 2)
    names = ("yh", "z", "c", "x", "yl")
    fine = Mesh(mesh.devices.reshape(shape), names)
    dp = ("yh", "z", "c")
    return jax.shard_map(
        functools.partial(body, dict(zip(names, shape))),
        mesh=fine,
        in_specs=(
            P(dp, TENSOR),
            P(dp, TENSOR),
            P(None, TENSOR),
            P(dp, None, TENSOR),
            P(None, TENSOR, None),
        ),
        out_specs=(P(dp, TENSOR), P(dp, None, TENSOR), P(None, TENSOR)),
        check_vma=False,
    )
```

time: 116 us -> 95.3 us (0.82)
  the two profiles are of different devices: /device:TPU:6 before, /device:TPU:1 now
where the time goes in v2:
time: 95.3 us; the launch traced here: 94.8 us
  starting transfers between devices  30.2 us (32%)
  waiting for transfers between devices  25.9 us (27%)
  Pallas kernels  22.4 us (24%)
  local copies, waits for them, and re-layouts  5.9 us (6%)
  other arithmetic  5.56 us (6%)
  matrix products  3.85 us (4%)
    all_to_all x1, waiting for transfers between devices, body(): got = lax.all_to_all(sent, TENSOR, 0, 0)  17.4 us
    ppermute x4, starting transfers between devices, exchange_sum(): return v + lax.ppermute(v, axes, [(i, i ^ move) for i in range(n)])  9.99 us
    all_to_all x1, starting transfers between devices, body(): got = lax.all_to_all(sent, TENSOR, 0, 0)  5.87 us
    unnamed x22, local copies, waits for them, and re-layouts  5.87 us
    add x1, other arithmetic, body(): new_momentum = rest + grad.astype(F32) * own_scale  5.31 us
    pallas_call x1, Pallas kernels, body(): pl.pallas_call(rest_kernel, in_specs=[VMEM, HBM, HBM], out_specs=HBM, out...  5.27 us
    ppermute x4, waiting for transfers between devices, exchange_sum(): return v + lax.ppermute(v, axes, [(i, i ^ move) for i in range(n)])  4.87 us
    all_to_all x1, starting transfers between devices, body(): grad = lax.all_to_all(grad, TENSOR, 0, 0)  4.35 us
  transfers between devices with their start and end apart: 12, of which 6 were waited for; matrix products, arithmetic and copies ran while one was open for 4% of the time, Pallas kernels for 21%

profile of v2, /device:TPU:1, one launch (start us, length us, event | category | flops | bytes accessed | tf_op | source)
XLA Modules:
  0.0 94.8 jit_solution(14735926040405060610)
XLA Ops:
  0.7 2.2 %gather_cotangent.1 = bf16[8,768,128]{2,1,0:T(8,128)(2,1)} custom-call(bf16[512,128]{1,0:T(8,128)(2,1)} %cot_hbm.1, bf16[8,1024,128]{2,1,0:T(8,128)(2,1)} %bitcast.13), custom_call_target="tpu_custom_call" | custom-call | flops 1000000 | bytes 2097152 | tf_op jit(solution)/shard_map/gather_cotangent/pallas_call | solution.py:383
  2.8 5.9 %all-to-all-start = ((bf16[8,768,128]{2,1,0:T(8,128)(2,1)}), bf16[8,768,128]{2,1,0:T(8,128)(2,1)S(1)}, u32[]{:S(2)}, u32[]{:S(2)}) async-start(bf16[8,768,128]{2,1,0:T(8,128)(2,1)} %gather_cotangent.1), calls=%async_computation | async-start | bytes 3145728 | tf_op jit(solution)/shard_map/gather_cotangent/all_to_all | solution.py:396
  8.7 4.2 %moment_band.1 = (f32[8,64,128]{2,1,0:T(8,128)S(1)}, bf16[2,256,512]{2,1,0:T(8,128)(2,1)S(1)}) custom-call(f32[8192,128]{1,0:T(8,128)} %bitcast.14, bf16[512,1024]{1,0:T(8,128)(2,1)} %a_hbm.1, s32[2,2,128]{2,1,0:T(2,128)S(1)} %bitcast.9, bf16[640,256]{1,0:T(8,128)(2,1)S(1)} %copy-done.5), custom_call_target="tpu_custom_call" | custom-call | flops 2000000000 | bytes 5242880 | tf_op jit(solution)/shard_map/moment_band/pallas_call | solution.py:399
  14.4 17.4 %all-to-all-done.cot_ref.cot_hbm = bf16[8,768,128]{2,1,0:T(8,128)(2,1)S(1)} async-done(((bf16[8,768,128]{2,1,0:T(8,128)(2,1)}), bf16[8,768,128]{2,1,0:T(8,128)(2,1)S(1)}, u32[]{:S(2)}, u32[]{:S(2)}) %all-to-all-start) | async-done | bytes 1572896 | tf_op jit(solution)/shard_map/gather_cotangent/all_to_all | solution.py:396
  31.8 1.7 %collective-permute-start.1 = (bf16[8,256,128]{2,1,0:T(8,128)(2,1)S(1)}, bf16[8,256,128]{2,1,0:T(8,128)(2,1)S(1)}, u32[]{:S(2)}, u32[]{:S(2)}) collective-permute-start(bf16[8,256,128]{2,1,0:T(8,128)(2,1)S(1)} %slice.7.refs_0_), channel_id=1, source_target_pairs={{0,16},{16,0},{32,48},{48,32},{64,80},{80,64},{96,112},{112,96},{1... | collective-permute-start | bytes 1572872 | tf_op jit(solution)/shard_map/weight_share/ppermute | solution.py:425
  33.5 1.9 %collective-permute-start = (bf16[8,256,128]{2,1,0:T(8,128)(2,1)S(1)}, bf16[8,256,128]{2,1,0:T(8,128)(2,1)S(1)}, u32[]{:S(2)}, u32[]{:S(2)}) collective-permute-start(bf16[8,256,128]{2,1,0:T(8,128)(2,1)S(1)} %slice.7.refs_0_), channel_id=1, source_target_pairs={{0,8},{8,0},{1,9},{9,1},{2,10},{10,2},{3,11},{11,3},{4,12},{12,4},... | collective-permute-start | bytes 1572872 | tf_op jit(solution)/shard_map/weight_share/ppermute | solution.py:423
  35.4 1.0 %copy-done.6 = bf16[640,256]{1,0:T(8,128)(2,1)S(1)} copy-done((bf16[640,256]{1,0:T(8,128)(2,1)S(1)}, bf16[640,256]{1,0:T(8,128)(2,1)}, u32[]{:S(2)}) %copy-start.6) | copy-done | bytes 327704
  36.4 1.0 %copy-done.9 = bf16[2,256,512]{2,1,0:T(8,128)(2,1)S(1)} copy-done((bf16[2,256,512]{2,1,0:T(8,128)(2,1)S(1)}, bf16[2,256,512]{2,1,0:T(8,128)(2,1)}, u32[]{:S(2)}) %copy-start.9) | copy-done | bytes 524312
  37.4 3.9 %grad_band.1 = f32[8,64,128]{2,1,0:T(8,128)S(1)} custom-call(bf16[2,256,512]{2,1,0:T(8,128)(2,1)S(1)} %copy-done.9, bf16[8,768,128]{2,1,0:T(8,128)(2,1)S(1)} %all-to-all-done.cot_ref.cot_hbm, bf16[640,256]{1,0:T(8,128)(2,1)S(1)} %copy-done.6), custom_call_target="tpu_custom_call" | custom-call | flops 2000000000 | bytes 2097152 | tf_op jit(solution)/shard_map/grad_band/pallas_call | solution.py:429
  42.1 3.4 %all-to-all-start.1 = ((f32[8,64,128]{2,1,0:T(8,128)}), f32[8,64,128]{2,1,0:T(8,128)S(1)}, u32[]{:S(2)}, u32[]{:S(2)}) async-start(f32[8,64,128]{2,1,0:T(8,128)} %copy-done.2), calls=%async_computation.1 | async-start | bytes 524288 | tf_op jit(solution)/shard_map/grad_band/all_to_all | solution.py:444
  46.4 3.9 %fusion = f16[8,1024,128]{2,1,0:T(8,128)(2,1)} fusion(f32[8,128]{1,0:T(8,128)S(1)} %maximum_divide_fusion, bf16[512,1024]{1,0:T(8,128)(2,1)} %a_hbm.1, bf16[8,768,128]{2,1,0:T(8,128)(2,1)S(1)} %all-to-all-done.cot_ref.cot_hbm), kind=kOutput, calls=%fused_computation.2 | convolution fusion | flops 1075838976 | bytes 4198400 | tf_op jit(solution)/shard_map/weight_grad/tf,jtc->fjc/dot_general | solution.py:450
  50.3 2.0 %all-to-all-done.1.grad_ref = f32[8,64,128]{2,1,0:T(8,128)S(1)} async-done(((f32[8,64,128]{2,1,0:T(8,128)}), f32[8,64,128]{2,1,0:T(8,128)S(1)}, u32[]{:S(2)}, u32[]{:S(2)}) %all-to-all-start.1) | async-done | bytes 262176 | tf_op jit(solution)/shard_map/grad_band/all_to_all | solution.py:444
  52.2 4.3 %all-to-all-start.2 = ((f16[8,1024,128]{2,1,0:T(8,128)(2,1)}), f16[8,1024,128]{2,1,0:T(8,128)(2,1)}, u32[]{:S(2)}, u32[]{:S(2)}) async-start(f16[8,1024,128]{2,1,0:T(8,128)(2,1)} %fusion), calls=%async_computation.2 | async-start | bytes 4194304 | tf_op jit(solution)/shard_map/weight_grad/all_to_all | solution.py:453
  56.6 0.9 copy-done.1
  60.3 5.3 %rest.1 = f32[8,1024,128]{2,1,0:T(8,128)} custom-call(f32[8,64,128]{2,1,0:T(8,128)} %copy-done.4, f32[8192,128]{1,0:T(8,128)} %bitcast.15, bf16[640,256]{1,0:T(8,128)(2,1)} %constant.12.clone.table_ref.table_hbm), custom_call_target="tpu_custom_call" | custom-call | flops 3000000000 | bytes 8388608 | tf_op jit(solution)/shard_map/rest/pallas_call | solution.py:472
  65.7 4.4 %collective-permute-start.5 = (f32[64,128]{1,0:T(8,128)S(1)}, f32[64,128]{1,0:T(8,128)S(1)}, u32[]{:S(2)}, u32[]{:S(2)}) collective-permute-start(f32[64,128]{1,0:T(8,128)S(1)} %add.19), channel_id=1, source_target_pairs={{0,48},{16,32},{32,16},{48,0},{64,112},{80,96},{96,80},{112,64},{1... | collective-permute-start | bytes 98312 | tf_op jit(solution)/shard_map/band_total/ppermute | solution.py:371
  70.1 4.2 %input_grad.1 = bf16[512,1024]{1,0:T(8,128)(2,1)} custom-call(bf16[8,768,128]{2,1,0:T(8,128)(2,1)S(1)} %all-to-all-done.cot_ref.cot_hbm, bf16[8,256,128]{2,1,0:T(8,128)(2,1)S(1)} %slice.7.refs_0_, bf16[8,256,128]{2,1,0:T(8,128)(2,1)S(1)} %collective-permute-done.refs_1_, bf16[8,256,128]{2,1,0:T(8,128)(2,1)S(1)} %collective-permute-done.1.refs_2_, ...), custom_call_target="tpu_custom_call" | custom-call | flops 1000000000 | bytes 4194304 | tf_op jit(solution)/shard_map/input_grad/pallas_call | solution.py:488
  74.3 2.9 %collective-permute-start.6 = (f32[64,128]{1,0:T(8,128)S(1)}, f32[64,128]{1,0:T(8,128)S(1)}, u32[]{:S(2)}, u32[]{:S(2)}) collective-permute-start(f32[64,128]{1,0:T(8,128)S(1)} %add.20), channel_id=1, source_target_pairs={{0,112},{16,96},{32,80},{48,64},{64,48},{80,32},{96,16},{112,0},{1... | collective-permute-start | bytes 98312 | tf_op jit(solution)/shard_map/band_total/ppermute | solution.py:371
  77.2 1.7 %collective-permute-done.6 = f32[64,128]{1,0:T(8,128)S(1)} collective-permute-done((f32[64,128]{1,0:T(8,128)S(1)}, f32[64,128]{1,0:T(8,128)S(1)}, u32[]{:S(2)}, u32[]{:S(2)}) %collective-permute-start.6) | collective-permute-done | bytes 32800 | tf_op jit(solution)/shard_map/band_total/ppermute | solution.py:371
  78.9 2.6 %collective-permute-start.7 = (f32[64,128]{1,0:T(8,128)S(1)}, f32[64,128]{1,0:T(8,128)S(1)}, u32[]{:S(2)}, u32[]{:S(2)}) collective-permute-start(f32[64,128]{1,0:T(8,128)S(1)} %add.22), channel_id=1, source_target_pairs={{0,128},{128,0},{1,129},{129,1},{2,130},{130,2},{3,131},{131,3},{4... | collective-permute-start | bytes 98312 | tf_op jit(solution)/shard_map/band_total/ppermute | solution.py:371
  81.6 3.2 %collective-permute-done.7 = f32[64,128]{1,0:T(8,128)S(1)} collective-permute-done((f32[64,128]{1,0:T(8,128)S(1)}, f32[64,128]{1,0:T(8,128)S(1)}, u32[]{:S(2)}, u32[]{:S(2)}) %collective-permute-start.7) | collective-permute-done | bytes 32800 | tf_op jit(solution)/shard_map/band_total/ppermute | solution.py:371
  84.8 1.4 %collective-permute-start.8 = (f32[64,128]{1,0:T(8,128)S(1)}, f32[64,128]{1,0:T(8,128)S(1)}, u32[]{:S(2)}, u32[]{:S(2)}) collective-permute-start(f32[64,128]{1,0:T(8,128)S(1)} %add.23.mine_ref), channel_id=1, source_target_pairs={{0,8},{8,0},{1,9},{9,1},{2,10},{10,2},{3,11},{11,3},{4,12},{12,4},... | collective-permute-start | bytes 98312 | tf_op jit(solution)/shard_map/new_momentum/ppermute | solution.py:513
  87.0 2.4 %weight_step.1 = bf16[8192,128]{1,0:T(8,128)(2,1)} custom-call(f32[64,128]{1,0:T(8,128)S(1)} %add.23.mine_ref, f32[64,128]{1,0:T(8,128)S(1)} %collective-permute-done.8.other_ref, s32[2,2,128]{2,1,0:T(2,128)S(1)} %bitcast.11, bf16[640,256]{1,0:T(8,128)(2,1)S(1)} %copy-done.7), custom_call_target="tpu_custom_call" | custom-call | flops 3000000000 | bytes 2097152 | tf_op jit(solution)/shard_map/weight_step/pallas_call | solution.py:517
  89.4 5.3 %multiply_add_fusion = f32[8,1024,128]{2,1,0:T(8,128)} fusion(f32[8,1024,128]{2,1,0:T(8,128)} %rest.1, f16[8,1024,128]{2,1,0:T(8,128)(2,1)} %all-to-all-done.2, f32[128]{0:T(128)S(1)} %maximum_multiply_fusion), kind=kLoop, calls=%fused_computation | loop fusion | flops 3145728 | bytes 10486272 | tf_op jit(solution)/shard_map/new_momentum/add | solution.py:514
  (41 shorter events, 6.9 us)
Async XLA Ops:
  0.6 8.1 %copy-start.5 = (bf16[640,256]{1,0:T(8,128)(2,1)S(1)}, bf16[640,256]{1,0:T(8,128)(2,1)}, u32[]{:S(2)}) copy-start(bf16[640,256]{1,0:T(8,128)(2,1)} %constant.12.clone.table_ref.table_hbm) | copy-start | bytes 983044
  0.6 8.1 %copy-start.3 = (s32[128,2,2]{0,2,1:T(2,128)S(1)}, s32[128,2,2]{0,2,1:T(2,128)}, u32[]{:S(2)}) copy-start(s32[128,2,2]{0,2,1:T(2,128)} %param.10) | copy-start | bytes 6148
  2.8 28.9 %all-to-all-start = ((bf16[8,768,128]{2,1,0:T(8,128)(2,1)}), bf16[8,768,128]{2,1,0:T(8,128)(2,1)S(1)}, u32[]{:S(2)}, u32[]{:S(2)}) async-start(bf16[8,768,128]{2,1,0:T(8,128)(2,1)} %gather_cotangent.1), calls=%async_computation | async-start | bytes 3145728 | tf_op jit(solution)/shard_map/gather_cotangent/all_to_all | solution.py:396
  12.9 0.7 copy-start
  13.6 0.8 copy-start.8
  31.8 13.9 %collective-permute-start.1 = (bf16[8,256,128]{2,1,0:T(8,128)(2,1)S(1)}, bf16[8,256,128]{2,1,0:T(8,128)(2,1)S(1)}, u32[]{:S(2)}, u32[]{:S(2)}) collective-permute-start(bf16[8,256,128]{2,1,0:T(8,128)(2,1)S(1)} %slice.7.refs_0_), channel_id=1, source_target_pairs={{0,16},{16,0},{32,48},{48,32},{64,80},{80,64},{96,112},{112,96},{1... | collective-permute-start | bytes 1572872 | tf_op jit(solution)/shard_map/weight_share/ppermute | solution.py:425
  33.5 18.7 %collective-permute-start = (bf16[8,256,128]{2,1,0:T(8,128)(2,1)S(1)}, bf16[8,256,128]{2,1,0:T(8,128)(2,1)S(1)}, u32[]{:S(2)}, u32[]{:S(2)}) collective-permute-start(bf16[8,256,128]{2,1,0:T(8,128)(2,1)S(1)} %slice.7.refs_0_), channel_id=1, source_target_pairs={{0,8},{8,0},{1,9},{9,1},{2,10},{10,2},{3,11},{11,3},{4,12},{12,4},... | collective-permute-start | bytes 1572872 | tf_op jit(solution)/shard_map/weight_share/ppermute | solution.py:423
  35.4 1.0 %copy-start.6 = (bf16[640,256]{1,0:T(8,128)(2,1)S(1)}, bf16[640,256]{1,0:T(8,128)(2,1)}, u32[]{:S(2)}) copy-start(bf16[640,256]{1,0:T(8,128)(2,1)} %constant.12.clone.table_ref.table_hbm) | copy-start | bytes 983044
  36.4 1.0 %copy-start.9 = (bf16[2,256,512]{2,1,0:T(8,128)(2,1)S(1)}, bf16[2,256,512]{2,1,0:T(8,128)(2,1)}, u32[]{:S(2)}) copy-start(bf16[2,256,512]{2,1,0:T(8,128)(2,1)} %copy-done.8) | copy-start | bytes 1572868
  41.3 0.7 copy-start.2
  42.1 10.2 %all-to-all-start.1 = ((f32[8,64,128]{2,1,0:T(8,128)}), f32[8,64,128]{2,1,0:T(8,128)S(1)}, u32[]{:S(2)}, u32[]{:S(2)}) async-start(f32[8,64,128]{2,1,0:T(8,128)} %copy-done.2), calls=%async_computation.1 | async-start | bytes 524288 | tf_op jit(solution)/shard_map/grad_band/all_to_all | solution.py:444
  45.7 6.6 %collective-permute-start.2 = (bf16[8,256,128]{2,1,0:T(8,128)(2,1)S(1)}, bf16[8,256,128]{2,1,0:T(8,128)(2,1)}, u32[]{:S(2)}, u32[]{:S(2)}) collective-permute-start(bf16[8,256,128]{2,1,0:T(8,128)(2,1)S(1)} %collective-permute-done.1.refs_2_), channel_id=1, source_target_pairs={{0,8},{8,0},{1,9},{9,1},{2,10},{10,2},{3,11},{11,3},{4,12},{12,4},... | collective-permute-start | bytes 1572872 | tf_op jit(solution)/shard_map/weight_share/ppermute | solution.py:426
  52.2 37.2 %all-to-all-start.2 = ((f16[8,1024,128]{2,1,0:T(8,128)(2,1)}), f16[8,1024,128]{2,1,0:T(8,128)(2,1)}, u32[]{:S(2)}, u32[]{:S(2)}) async-start(f16[8,1024,128]{2,1,0:T(8,128)(2,1)} %fusion), calls=%async_computation.2 | async-start | bytes 4194304 | tf_op jit(solution)/shard_map/weight_grad/all_to_all | solution.py:453
  56.6 1.0 %copy-start.1 = (f32[8,64,128]{2,1,0:T(8,128)S(1)}, f32[8,64,128]{2,1,0:T(8,128)}, u32[]{:S(2)}) copy-start(f32[8,64,128]{2,1,0:T(8,128)} %copy-done) | copy-start | bytes 786436
  57.9 0.7 copy-start.4
  58.7 1.7 %collective-permute-start.3 = (f32[64,128]{1,0:T(8,128)S(1)}, f32[64,128]{1,0:T(8,128)S(1)}, u32[]{:S(2)}, u32[]{:S(2)}) collective-permute-start(f32[64,128]{1,0:T(8,128)S(1)} %get-tuple-element.32), channel_id=1, source_target_pairs={{0,8},{8,0},{1,9},{9,1},{2,10},{10,2},{3,11},{11,3},{4,12},{12,4},... | collective-permute-start | bytes 98312 | tf_op jit(solution)/shard_map/band_total/ppermute | solution.py:504
  60.3 5.3 %collective-permute-start.4 = (f32[64,128]{1,0:T(8,128)S(1)}, f32[64,128]{1,0:T(8,128)S(1)}, u32[]{:S(2)}, u32[]{:S(2)}) collective-permute-start(f32[64,128]{1,0:T(8,128)S(1)} %add.18), channel_id=1, source_target_pairs={{0,16},{16,0},{32,48},{48,32},{64,80},{80,64},{96,112},{112,96},{1... | collective-permute-start | bytes 98312 | tf_op jit(solution)/shard_map/band_total/ppermute | solution.py:371
  65.6 15.9 %copy-start.10 = (bf16[512,128]{1,0:T(8,128)(2,1)S(1)}, bf16[512,128]{1,0:T(8,128)(2,1)}, u32[]{:S(2)}) copy-start(bf16[512,128]{1,0:T(8,128)(2,1)} %cot_hbm.1) | copy-start | bytes 393220
  65.6 21.4 %copy-start.7 = (bf16[640,256]{1,0:T(8,128)(2,1)S(1)}, bf16[640,256]{1,0:T(8,128)(2,1)}, u32[]{:S(2)}) copy-start(bf16[640,256]{1,0:T(8,128)(2,1)} %constant.12.clone.table_ref.table_hbm) | copy-start | bytes 983044
  65.7 8.6 %collective-permute-start.5 = (f32[64,128]{1,0:T(8,128)S(1)}, f32[64,128]{1,0:T(8,128)S(1)}, u32[]{:S(2)}, u32[]{:S(2)}) collective-permute-start(f32[64,128]{1,0:T(8,128)S(1)} %add.19), channel_id=1, source_target_pairs={{0,48},{16,32},{32,16},{48,0},{64,112},{80,96},{96,80},{112,64},{1... | collective-permute-start | bytes 98312 | tf_op jit(solution)/shard_map/band_total/ppermute | solution.py:371
  74.3 4.6 %collective-permute-start.6 = (f32[64,128]{1,0:T(8,128)S(1)}, f32[64,128]{1,0:T(8,128)S(1)}, u32[]{:S(2)}, u32[]{:S(2)}) collective-permute-start(f32[64,128]{1,0:T(8,128)S(1)} %add.20), channel_id=1, source_target_pairs={{0,112},{16,96},{32,80},{48,64},{64,48},{80,32},{96,16},{112,0},{1... | collective-permute-start | bytes 98312 | tf_op jit(solution)/shard_map/band_total/ppermute | solution.py:371
  78.9 5.8 %collective-permute-start.7 = (f32[64,128]{1,0:T(8,128)S(1)}, f32[64,128]{1,0:T(8,128)S(1)}, u32[]{:S(2)}, u32[]{:S(2)}) collective-permute-start(f32[64,128]{1,0:T(8,128)S(1)} %add.22), channel_id=1, source_target_pairs={{0,128},{128,0},{1,129},{129,1},{2,130},{130,2},{3,131},{131,3},{4... | collective-permute-start | bytes 98312 | tf_op jit(solution)/shard_map/band_total/ppermute | solution.py:371
  84.8 2.3 %collective-permute-start.8 = (f32[64,128]{1,0:T(8,128)S(1)}, f32[64,128]{1,0:T(8,128)S(1)}, u32[]{:S(2)}, u32[]{:S(2)}) collective-permute-start(f32[64,128]{1,0:T(8,128)S(1)} %add.23.mine_ref), channel_id=1, source_target_pairs={{0,8},{8,0},{1,9},{9,1},{2,10},{10,2},{3,11},{11,3},{4,12},{12,4},... | collective-permute-start | bytes 98312 | tf_op jit(solution)/shard_map/new_momentum/ppermute | solution.py:513

commit v3 on v2

--- a/solution.py
+++ b/solution.py
@@ -183,15 +183,7 @@
     return mine
 
 
-def grad_band_kernel(act_hbm, cot_ref, table_hbm, o_hbm, *scratch):
-    act_ref, table_ref, out, sems = scratch
-    get_table = pltpu.make_async_copy(table_hbm.at[COLS], table_ref, sems.at[0])
-    get_act = pltpu.make_async_copy(act_hbm, act_ref, sems.at[1])
-    put = []
-    for copy in (get_table, get_act):
-        copy.start()
-    get_table.wait()
-    get_act.wait()
+def grad_band_kernel(act_ref, cot_ref, table_ref, out):
     high, low = act_ref[0], act_ref[1]
     for j in range(0, 8, 2):
         halves = []
@@ -209,11 +201,6 @@
                         for kk in range(4)
                     ]
                 )
-        two = pl.ds(j, 2)
-        put.append(pltpu.make_async_copy(out.at[two], o_hbm.at[two], sems.at[5 + j // 2]))
-        put[-1].start()
-    for copy in put:
-        copy.wait()
 
 
 def pack_kernel(moment_hbm, grad_ref, anchor_ref, low_ref, keep_ref, give_ref, *scratch):
@@ -428,18 +415,10 @@
     with jax.named_scope("grad_band"):
         grad_band = pl.pallas_call(
             grad_band_kernel,
-            in_specs=[HBM, VMEM, HBM],
-            out_specs=HBM,
             out_shape=jax.ShapeDtypeStruct((8, 64, 128), F32),
-            scratch_shapes=[
-                pltpu.VMEM((2, 256, 512), BF16),
-                pltpu.VMEM((128, 256), BF16),
-                pltpu.VMEM((8, 64, 128), F32),
-                pltpu.SemaphoreType.DMA((9,)),
-            ],
-            compiler_params=params(40),
+            compiler_params=params(24),
             cost_estimate=cost(2000, 2048),
-        )(act_band, got, table)
+        )(act_band, got, jnp.asarray(tables()[COLS]))
         got, grad_band = lax.optimization_barrier((got, grad_band))
         grad_band = lax.all_to_all(grad_band, TENSOR, 0, 0)
 
@@ -480,7 +459,7 @@
                 pltpu.VMEM((8, 2, 192, 256), BF16),
                 pltpu.SemaphoreType.DMA((18,)),
             ],
-            compiler_params=params(56),
+            compiler_params=params(52),
             cost_estimate=cost(3000, 8192),
         )(low, moment0, table)
 

time: 95.3 us -> 93.4 us (0.980)
  Pallas kernels: 22.4 us -> 18.8 us
  waiting for transfers between devices: 25.9 us -> 27.8 us
    pallas_call x1, Pallas kernels: 3.9 us -> 1.69 us  [body(): pl.pallas_call(grad_band_kernel, out_shape=jax.ShapeDtypeStruct((8, 64, 1...]
    ppermute x4, waiting for transfers between devices: 4.87 us -> 6.85 us  [exchange_sum(): return v + lax.ppermute(v, axes, [(i, i ^ move) for i in range(n)])]
    all_to_all x1, waiting for transfers between devices: 1.98 us -> 0.01 us  [body(): grad_band = lax.all_to_all(grad_band, TENSOR, 0, 0)]
    ppermute x1, starting transfers between devices: 0.74 us -> 2.37 us  [body(): shares += [share, lax.ppermute(share, 'c', swap)]]
    ppermute x1, waiting for transfers between devices: 0.01 us -> 1.57 us  [body(): share = lax.ppermute(share, 'z', [(k, k ^ 1) for k in range(nz)])]
    pallas_call x1, Pallas kernels: 5.27 us -> 3.86 us  [body(): pl.pallas_call(rest_kernel, in_specs=[VMEM, HBM, HBM], out_specs=HBM, out...]
    ppermute x1, starting transfers between devices: 1.43 us -> 0.39 us  [body(): other = lax.ppermute(mine, 'c', swap)]
    unnamed x22 -> x20, local copies, waits for them, and re-layouts: 5.87 us -> 5.17 us
  transfers between devices with their start and end apart: 12 -> 12, of which waited for: 6 -> 6; matrix products, arithmetic and copies ran while one was open for 4% -> 4% of each run, Pallas kernels for 21% -> 18%
where the time goes in v3:
time: 93.4 us; the launch traced here: 92.9 us
  starting transfers between devices  30.8 us (33%)
  waiting for transfers between devices  27.8 us (30%)
  Pallas kernels  18.8 us (20%)
  other arithmetic  5.56 us (6%)
  local copies, waits for them, and re-layouts  5.21 us (6%)
  matrix products  3.86 us (4%)
    all_to_all x1, waiting for transfers between devices, body(): got = lax.all_to_all(sent, TENSOR, 0, 0)  17.3 us
    ppermute x4, starting transfers between devices, exchange_sum(): return v + lax.ppermute(v, axes, [(i, i ^ move) for i in range(n)])  10.7 us
    ppermute x4, waiting for transfers between devices, exchange_sum(): return v + lax.ppermute(v, axes, [(i, i ^ move) for i in range(n)])  6.85 us
    all_to_all x1, starting transfers between devices, body(): got = lax.all_to_all(sent, TENSOR, 0, 0)  5.87 us
    add x1, other arithmetic, body(): new_momentum = rest + grad.astype(F32) * own_scale  5.31 us
    unnamed x20, local copies, waits for them, and re-layouts  5.17 us
    all_to_all x1, starting transfers between devices, body(): grad = lax.all_to_all(grad, TENSOR, 0, 0)  4.35 us
    pallas_call x1, Pallas kernels, body(): pl.pallas_call(moment_band_kernel, in_specs=[HBM, HBM, VMEM, VMEM], out_s...  4.19 us
  transfers between devices with their start and end apart: 12, of which 6 were waited for; matrix products, arithmetic and copies ran while one was open for 4% of the time, Pallas kernels for 18%

profile of v3, /device:TPU:1, one launch (start us, length us, event | category | flops | bytes accessed | tf_op | source)
XLA Modules:
  0.0 92.9 jit_solution(13401443432740030842)
XLA Ops:
  0.7 2.2 %gather_cotangent.1 = bf16[8,768,128]{2,1,0:T(8,128)(2,1)} custom-call(bf16[512,128]{1,0:T(8,128)(2,1)} %cot_hbm.1, bf16[8,1024,128]{2,1,0:T(8,128)(2,1)} %bitcast.13), custom_call_target="tpu_custom_call" | custom-call | flops 1000000 | bytes 2097152 | tf_op jit(solution)/shard_map/gather_cotangent/pallas_call | solution.py:370
  2.8 5.9 %all-to-all-start = ((bf16[8,768,128]{2,1,0:T(8,128)(2,1)}), bf16[8,768,128]{2,1,0:T(8,128)(2,1)S(1)}, u32[]{:S(2)}, u32[]{:S(2)}) async-start(bf16[8,768,128]{2,1,0:T(8,128)(2,1)} %gather_cotangent.1), calls=%async_computation | async-start | bytes 3145728 | tf_op jit(solution)/shard_map/gather_cotangent/all_to_all | solution.py:383
  8.7 4.2 %moment_band.1 = (f32[8,64,128]{2,1,0:T(8,128)S(1)}, bf16[2,256,512]{2,1,0:T(8,128)(2,1)S(1)}) custom-call(f32[8192,128]{1,0:T(8,128)} %bitcast.14, bf16[512,1024]{1,0:T(8,128)(2,1)} %a_hbm.1, s32[2,2,128]{2,1,0:T(2,128)S(1)} %bitcast.9, bf16[640,256]{1,0:T(8,128)(2,1)S(1)} %copy-done.4), custom_call_target="tpu_custom_call" | custom-call | flops 2000000000 | bytes 5242880 | tf_op jit(solution)/shard_map/moment_band/pallas_call | solution.py:386
  14.4 17.3 %all-to-all-done.cot_ref.cot_hbm = bf16[8,768,128]{2,1,0:T(8,128)(2,1)S(1)} async-done(((bf16[8,768,128]{2,1,0:T(8,128)(2,1)}), bf16[8,768,128]{2,1,0:T(8,128)(2,1)S(1)}, u32[]{:S(2)}, u32[]{:S(2)}) %all-to-all-start) | async-done | bytes 1572896 | tf_op jit(solution)/shard_map/gather_cotangent/all_to_all | solution.py:383
  31.8 1.7 %collective-permute-start.1 = (bf16[8,256,128]{2,1,0:T(8,128)(2,1)S(1)}, bf16[8,256,128]{2,1,0:T(8,128)(2,1)S(1)}, u32[]{:S(2)}, u32[]{:S(2)}) collective-permute-start(bf16[8,256,128]{2,1,0:T(8,128)(2,1)S(1)} %slice.7.refs_0_), channel_id=1, source_target_pairs={{0,16},{16,0},{32,48},{48,32},{64,80},{80,64},{96,112},{112,96},{1... | collective-permute-start | bytes 1572872 | tf_op jit(solution)/shard_map/weight_share/ppermute | solution.py:412
  33.5 1.9 %collective-permute-start = (bf16[8,256,128]{2,1,0:T(8,128)(2,1)S(1)}, bf16[8,256,128]{2,1,0:T(8,128)(2,1)S(1)}, u32[]{:S(2)}, u32[]{:S(2)}) collective-permute-start(bf16[8,256,128]{2,1,0:T(8,128)(2,1)S(1)} %slice.7.refs_0_), channel_id=1, source_target_pairs={{0,8},{8,0},{1,9},{9,1},{2,10},{10,2},{3,11},{11,3},{4,12},{12,4},... | collective-permute-start | bytes 1572872 | tf_op jit(solution)/shard_map/weight_share/ppermute | solution.py:410
  35.4 1.0 %copy-done.8 = bf16[2,256,512]{2,1,0:T(8,128)(2,1)S(1)} copy-done((bf16[2,256,512]{2,1,0:T(8,128)(2,1)S(1)}, bf16[2,256,512]{2,1,0:T(8,128)(2,1)}, u32[]{:S(2)}) %copy-start.8) | copy-done | bytes 524312
  36.5 1.7 %grad_band.1 = f32[8,64,128]{2,1,0:T(8,128)S(1)} custom-call(bf16[2,256,512]{2,1,0:T(8,128)(2,1)S(1)} %copy-done.8, bf16[8,768,128]{2,1,0:T(8,128)(2,1)S(1)} %all-to-all-done.cot_ref.cot_hbm, bf16[128,256]{1,0:T(8,128)(2,1)S(1)} %copy-done.6), custom_call_target="tpu_custom_call" | custom-call | flops 2000000000 | bytes 2097152 | tf_op jit(solution)/shard_map/grad_band/pallas_call | solution.py:416
  38.9 3.4 %all-to-all-start.1 = ((f32[8,64,128]{2,1,0:T(8,128)}), f32[8,64,128]{2,1,0:T(8,128)S(1)}, u32[]{:S(2)}, u32[]{:S(2)}) async-start(f32[8,64,128]{2,1,0:T(8,128)} %copy-done.2), calls=%async_computation.1 | async-start | bytes 524288 | tf_op jit(solution)/shard_map/grad_band/all_to_all | solution.py:423
  42.5 1.6 %collective-permute-done.1.refs_2_ = bf16[8,256,128]{2,1,0:T(8,128)(2,1)S(1)} collective-permute-done((bf16[8,256,128]{2,1,0:T(8,128)(2,1)S(1)}, bf16[8,256,128]{2,1,0:T(8,128)(2,1)S(1)}, u32[]{:S(2)}, u32[]{:S(2)}) %collective-permute-start.1) | collective-permute-done | bytes 524320 | tf_op jit(solution)/shard_map/weight_share/ppermute | solution.py:412
  44.0 2.4 %collective-permute-start.2 = (bf16[8,256,128]{2,1,0:T(8,128)(2,1)S(1)}, bf16[8,256,128]{2,1,0:T(8,128)(2,1)}, u32[]{:S(2)}, u32[]{:S(2)}) collective-permute-start(bf16[8,256,128]{2,1,0:T(8,128)(2,1)S(1)} %collective-permute-done.1.refs_2_), channel_id=1, source_target_pairs={{0,8},{8,0},{1,9},{9,1},{2,10},{10,2},{3,11},{11,3},{4,12},{12,4},... | collective-permute-start | bytes 1572872 | tf_op jit(solution)/shard_map/weight_share/ppermute | solution.py:413
  46.4 3.9 %fusion = f16[8,1024,128]{2,1,0:T(8,128)(2,1)} fusion(f32[8,128]{1,0:T(8,128)S(1)} %maximum_divide_fusion, bf16[512,1024]{1,0:T(8,128)(2,1)} %a_hbm.1, bf16[8,768,128]{2,1,0:T(8,128)(2,1)S(1)} %all-to-all-done.cot_ref.cot_hbm), kind=kOutput, calls=%fused_computation.2 | convolution fusion | flops 1075838976 | bytes 4198400 | tf_op jit(solution)/shard_map/weight_grad/tf,jtc->fjc/dot_general | solution.py:429
  50.3 4.4 %all-to-all-start.2 = ((f16[8,1024,128]{2,1,0:T(8,128)(2,1)}), f16[8,1024,128]{2,1,0:T(8,128)(2,1)}, u32[]{:S(2)}, u32[]{:S(2)}) async-start(f16[8,1024,128]{2,1,0:T(8,128)(2,1)} %fusion), calls=%async_computation.2 | async-start | bytes 4194304 | tf_op jit(solution)/shard_map/weight_grad/all_to_all | solution.py:432
  56.1 1.2 %collective-permute-done.3 = f32[64,128]{1,0:T(8,128)S(1)} collective-permute-done((f32[64,128]{1,0:T(8,128)S(1)}, f32[64,128]{1,0:T(8,128)S(1)}, u32[]{:S(2)}, u32[]{:S(2)}) %collective-permute-start.3) | collective-permute-done | bytes 32800 | tf_op jit(solution)/shard_map/band_total/ppermute | solution.py:483
  57.3 1.5 %collective-permute-start.4 = (f32[64,128]{1,0:T(8,128)S(1)}, f32[64,128]{1,0:T(8,128)S(1)}, u32[]{:S(2)}, u32[]{:S(2)}) collective-permute-start(f32[64,128]{1,0:T(8,128)S(1)} %add.18), channel_id=1, source_target_pairs={{0,16},{16,0},{32,48},{48,32},{64,80},{80,64},{96,112},{112,96},{1... | collective-permute-start | bytes 98312 | tf_op jit(solution)/shard_map/band_total/ppermute | solution.py:358
  59.7 3.9 %rest.1 = f32[8,1024,128]{2,1,0:T(8,128)} custom-call(f32[8,64,128]{2,1,0:T(8,128)S(1)} %get-tuple-element.33.low_ref, f32[8192,128]{1,0:T(8,128)} %bitcast.15, bf16[640,256]{1,0:T(8,128)(2,1)S(1)} %copy-done.5), custom_call_target="tpu_custom_call" | custom-call | flops 3000000000 | bytes 8388608 | tf_op jit(solution)/shard_map/rest/pallas_call | solution.py:451
  63.6 3.0 %collective-permute-start.5 = (f32[64,128]{1,0:T(8,128)S(1)}, f32[64,128]{1,0:T(8,128)S(1)}, u32[]{:S(2)}, u32[]{:S(2)}) collective-permute-start(f32[64,128]{1,0:T(8,128)S(1)} %add.19), channel_id=1, source_target_pairs={{0,48},{16,32},{32,16},{48,0},{64,112},{80,96},{96,80},{112,64},{1... | collective-permute-start | bytes 98312 | tf_op jit(solution)/shard_map/band_total/ppermute | solution.py:358
  66.6 4.2 %input_grad.1 = bf16[512,1024]{1,0:T(8,128)(2,1)} custom-call(bf16[8,768,128]{2,1,0:T(8,128)(2,1)S(1)} %all-to-all-done.cot_ref.cot_hbm, bf16[8,256,128]{2,1,0:T(8,128)(2,1)S(1)} %slice.7.refs_0_, bf16[8,256,128]{2,1,0:T(8,128)(2,1)S(1)} %collective-permute-done.refs_1_, bf16[8,256,128]{2,1,0:T(8,128)(2,1)S(1)} %collective-permute-done.1.refs_2_, ...), custom_call_target="tpu_custom_call" | custom-call | flops 1000000000 | bytes 4194304 | tf_op jit(solution)/shard_map/input_grad/pallas_call | solution.py:467
  70.8 3.7 %collective-permute-start.6 = (f32[64,128]{1,0:T(8,128)S(1)}, f32[64,128]{1,0:T(8,128)S(1)}, u32[]{:S(2)}, u32[]{:S(2)}) collective-permute-start(f32[64,128]{1,0:T(8,128)S(1)} %add.20), channel_id=1, source_target_pairs={{0,112},{16,96},{32,80},{48,64},{64,48},{80,32},{96,16},{112,0},{1... | collective-permute-start | bytes 98312 | tf_op jit(solution)/shard_map/band_total/ppermute | solution.py:358
  74.5 1.7 %collective-permute-done.6 = f32[64,128]{1,0:T(8,128)S(1)} collective-permute-done((f32[64,128]{1,0:T(8,128)S(1)}, f32[64,128]{1,0:T(8,128)S(1)}, u32[]{:S(2)}, u32[]{:S(2)}) %collective-permute-start.6) | collective-permute-done | bytes 32800 | tf_op jit(solution)/shard_map/band_total/ppermute | solution.py:358
  76.2 2.6 %collective-permute-start.7 = (f32[64,128]{1,0:T(8,128)S(1)}, f32[64,128]{1,0:T(8,128)S(1)}, u32[]{:S(2)}, u32[]{:S(2)}) collective-permute-start(f32[64,128]{1,0:T(8,128)S(1)} %add.22), channel_id=1, source_target_pairs={{0,128},{128,0},{1,129},{129,1},{2,130},{130,2},{3,131},{131,3},{4... | collective-permute-start | bytes 98312 | tf_op jit(solution)/shard_map/band_total/ppermute | solution.py:358
  78.8 5.1 %collective-permute-done.7 = f32[64,128]{1,0:T(8,128)S(1)} collective-permute-done((f32[64,128]{1,0:T(8,128)S(1)}, f32[64,128]{1,0:T(8,128)S(1)}, u32[]{:S(2)}, u32[]{:S(2)}) %collective-permute-start.7) | collective-permute-done | bytes 32800 | tf_op jit(solution)/shard_map/band_total/ppermute | solution.py:358
  85.2 2.4 %weight_step.1 = bf16[8192,128]{1,0:T(8,128)(2,1)} custom-call(f32[64,128]{1,0:T(8,128)S(1)} %add.23.mine_ref, f32[64,128]{1,0:T(8,128)S(1)} %collective-permute-done.8.other_ref, s32[2,2,128]{2,1,0:T(2,128)S(1)} %bitcast.11, bf16[640,256]{1,0:T(8,128)(2,1)S(1)} %copy-done.5), custom_call_target="tpu_custom_call" | custom-call | flops 3000000000 | bytes 2097152 | tf_op jit(solution)/shard_map/weight_step/pallas_call | solution.py:496
  87.6 5.3 %multiply_add_fusion = f32[8,1024,128]{2,1,0:T(8,128)} fusion(f32[8,1024,128]{2,1,0:T(8,128)} %rest.1, f16[8,1024,128]{2,1,0:T(8,128)(2,1)} %all-to-all-done.2, f32[128]{0:T(128)S(1)} %maximum_multiply_fusion), kind=kLoop, calls=%fused_computation | loop fusion | flops 3145728 | bytes 10486272 | tf_op jit(solution)/shard_map/new_momentum/add | solution.py:493
  (39 shorter events, 6.1 us)
Async XLA Ops:
  0.6 8.1 %copy-start.4 = (bf16[640,256]{1,0:T(8,128)(2,1)S(1)}, bf16[640,256]{1,0:T(8,128)(2,1)}, u32[]{:S(2)}) copy-start(bf16[640,256]{1,0:T(8,128)(2,1)} %constant.14.clone.table_ref.table_hbm) | copy-start | bytes 983044
  0.6 8.1 %copy-start.3 = (s32[128,2,2]{0,2,1:T(2,128)S(1)}, s32[128,2,2]{0,2,1:T(2,128)}, u32[]{:S(2)}) copy-start(s32[128,2,2]{0,2,1:T(2,128)} %param.11) | copy-start | bytes 6148
  2.8 28.9 %all-to-all-start = ((bf16[8,768,128]{2,1,0:T(8,128)(2,1)}), bf16[8,768,128]{2,1,0:T(8,128)(2,1)S(1)}, u32[]{:S(2)}, u32[]{:S(2)}) async-start(bf16[8,768,128]{2,1,0:T(8,128)(2,1)} %gather_cotangent.1), calls=%async_computation | async-start | bytes 3145728 | tf_op jit(solution)/shard_map/gather_cotangent/all_to_all | solution.py:383
  8.7 26.7 %copy-start.6 = (bf16[128,256]{1,0:T(8,128)(2,1)S(1)}, bf16[128,256]{1,0:T(8,128)(2,1)}, u32[]{:S(2)}) copy-start(bf16[128,256]{1,0:T(8,128)(2,1)} %constant.15.clone.table_ref) | copy-start | bytes 196612
  12.9 0.7 copy-start
  13.7 0.8 copy-start.7
  31.8 12.2 %collective-permute-start.1 = (bf16[8,256,128]{2,1,0:T(8,128)(2,1)S(1)}, bf16[8,256,128]{2,1,0:T(8,128)(2,1)S(1)}, u32[]{:S(2)}, u32[]{:S(2)}) collective-permute-start(bf16[8,256,128]{2,1,0:T(8,128)(2,1)S(1)} %slice.7.refs_0_), channel_id=1, source_target_pairs={{0,16},{16,0},{32,48},{48,32},{64,80},{80,64},{96,112},{112,96},{1... | collective-permute-start | bytes 1572872 | tf_op jit(solution)/shard_map/weight_share/ppermute | solution.py:412
  33.5 16.8 %collective-permute-start = (bf16[8,256,128]{2,1,0:T(8,128)(2,1)S(1)}, bf16[8,256,128]{2,1,0:T(8,128)(2,1)S(1)}, u32[]{:S(2)}, u32[]{:S(2)}) collective-permute-start(bf16[8,256,128]{2,1,0:T(8,128)(2,1)S(1)} %slice.7.refs_0_), channel_id=1, source_target_pairs={{0,8},{8,0},{1,9},{9,1},{2,10},{10,2},{3,11},{11,3},{4,12},{12,4},... | collective-permute-start | bytes 1572872 | tf_op jit(solution)/shard_map/weight_share/ppermute | solution.py:410
  35.4 1.0 %copy-start.8 = (bf16[2,256,512]{2,1,0:T(8,128)(2,1)S(1)}, bf16[2,256,512]{2,1,0:T(8,128)(2,1)}, u32[]{:S(2)}) copy-start(bf16[2,256,512]{2,1,0:T(8,128)(2,1)} %copy-done.7) | copy-start | bytes 1572868
  38.2 0.7 copy-start.2
  38.9 11.4 %all-to-all-start.1 = ((f32[8,64,128]{2,1,0:T(8,128)}), f32[8,64,128]{2,1,0:T(8,128)S(1)}, u32[]{:S(2)}, u32[]{:S(2)}) async-start(f32[8,64,128]{2,1,0:T(8,128)} %copy-done.2), calls=%async_computation.1 | async-start | bytes 524288 | tf_op jit(solution)/shard_map/grad_band/all_to_all | solution.py:423
  44.0 6.2 %collective-permute-start.2 = (bf16[8,256,128]{2,1,0:T(8,128)(2,1)S(1)}, bf16[8,256,128]{2,1,0:T(8,128)(2,1)}, u32[]{:S(2)}, u32[]{:S(2)}) collective-permute-start(bf16[8,256,128]{2,1,0:T(8,128)(2,1)S(1)} %collective-permute-done.1.refs_2_), channel_id=1, source_target_pairs={{0,8},{8,0},{1,9},{9,1},{2,10},{10,2},{3,11},{11,3},{4,12},{12,4},... | collective-permute-start | bytes 1572872 | tf_op jit(solution)/shard_map/weight_share/ppermute | solution.py:413
  50.3 37.3 %all-to-all-start.2 = ((f16[8,1024,128]{2,1,0:T(8,128)(2,1)}), f16[8,1024,128]{2,1,0:T(8,128)(2,1)}, u32[]{:S(2)}, u32[]{:S(2)}) async-start(f16[8,1024,128]{2,1,0:T(8,128)(2,1)} %fusion), calls=%async_computation.2 | async-start | bytes 4194304 | tf_op jit(solution)/shard_map/weight_grad/all_to_all | solution.py:432
  54.6 1.0 %copy-start.1 = (f32[8,64,128]{2,1,0:T(8,128)S(1)}, f32[8,64,128]{2,1,0:T(8,128)}, u32[]{:S(2)}) copy-start(f32[8,64,128]{2,1,0:T(8,128)} %copy-done) | copy-start | bytes 786436
  56.0 1.3 %collective-permute-start.3 = (f32[64,128]{1,0:T(8,128)S(1)}, f32[64,128]{1,0:T(8,128)S(1)}, u32[]{:S(2)}, u32[]{:S(2)}) collective-permute-start(f32[64,128]{1,0:T(8,128)S(1)} %get-tuple-element.32), channel_id=1, source_target_pairs={{0,8},{8,0},{1,9},{9,1},{2,10},{10,2},{3,11},{11,3},{4,12},{12,4},... | collective-permute-start | bytes 98312 | tf_op jit(solution)/shard_map/band_total/ppermute | solution.py:483
  57.3 6.3 %collective-permute-start.4 = (f32[64,128]{1,0:T(8,128)S(1)}, f32[64,128]{1,0:T(8,128)S(1)}, u32[]{:S(2)}, u32[]{:S(2)}) collective-permute-start(f32[64,128]{1,0:T(8,128)S(1)} %add.18), channel_id=1, source_target_pairs={{0,16},{16,0},{32,48},{48,32},{64,80},{80,64},{96,112},{112,96},{1... | collective-permute-start | bytes 98312 | tf_op jit(solution)/shard_map/band_total/ppermute | solution.py:358
  58.7 1.0 %copy-start.5 = (bf16[640,256]{1,0:T(8,128)(2,1)S(1)}, bf16[640,256]{1,0:T(8,128)(2,1)}, u32[]{:S(2)}) copy-start(bf16[640,256]{1,0:T(8,128)(2,1)} %constant.14.clone.table_ref.table_hbm) | copy-start | bytes 983044
  63.6 15.2 %copy-start.9 = (bf16[512,128]{1,0:T(8,128)(2,1)S(1)}, bf16[512,128]{1,0:T(8,128)(2,1)}, u32[]{:S(2)}) copy-start(bf16[512,128]{1,0:T(8,128)(2,1)} %cot_hbm.1) | copy-start | bytes 393220
  63.6 7.2 %collective-permute-start.5 = (f32[64,128]{1,0:T(8,128)S(1)}, f32[64,128]{1,0:T(8,128)S(1)}, u32[]{:S(2)}, u32[]{:S(2)}) collective-permute-start(f32[64,128]{1,0:T(8,128)S(1)} %add.19), channel_id=1, source_target_pairs={{0,48},{16,32},{32,16},{48,0},{64,112},{80,96},{96,80},{112,64},{1... | collective-permute-start | bytes 98312 | tf_op jit(solution)/shard_map/band_total/ppermute | solution.py:358
  70.8 5.4 %collective-permute-start.6 = (f32[64,128]{1,0:T(8,128)S(1)}, f32[64,128]{1,0:T(8,128)S(1)}, u32[]{:S(2)}, u32[]{:S(2)}) collective-permute-start(f32[64,128]{1,0:T(8,128)S(1)} %add.20), channel_id=1, source_target_pairs={{0,112},{16,96},{32,80},{48,64},{64,48},{80,32},{96,16},{112,0},{1... | collective-permute-start | bytes 98312 | tf_op jit(solution)/shard_map/band_total/ppermute | solution.py:358
  76.2 7.8 %collective-permute-start.7 = (f32[64,128]{1,0:T(8,128)S(1)}, f32[64,128]{1,0:T(8,128)S(1)}, u32[]{:S(2)}, u32[]{:S(2)}) collective-permute-start(f32[64,128]{1,0:T(8,128)S(1)} %add.22), channel_id=1, source_target_pairs={{0,128},{128,0},{1,129},{129,1},{2,130},{130,2},{3,131},{131,3},{4... | collective-permute-start | bytes 98312 | tf_op jit(solution)/shard_map/band_total/ppermute | solution.py:358
  84.0 1.2 %collective-permute-start.8 = (f32[64,128]{1,0:T(8,128)S(1)}, f32[64,128]{1,0:T(8,128)S(1)}, u32[]{:S(2)}, u32[]{:S(2)}) collective-permute-start(f32[64,128]{1,0:T(8,128)S(1)} %add.23.mine_ref), channel_id=1, source_target_pairs={{0,8},{8,0},{1,9},{9,1},{2,10},{10,2},{3,11},{11,3},{4,12},{12,4},... | collective-permute-start | bytes 98312 | tf_op jit(solution)/shard_map/new_momentum/ppermute | solution.py:492
